TPU v7x, 128 devices: a whole 4x4x4 slice. The times are simulated.
128 devices in a mesh: ctx: 8 (over y, core), vocab: 16 (over z, x).
Axes of the slice: x: 4, y: 4, z: 4, core: 2. Of those that a mesh axis runs over, the one named last changes fastest.
Arguments:
- queries: bfloat16 [4096, 4096], P('ctx', 'vocab')
- key_rows: bfloat16 [4096, 512], P('ctx')
- value_rows: bfloat16 [4096, 512], P('ctx'), may hold values from -6 to 6
- sink_logits: float32 [64], P('vocab'), may hold values from -6 to 6
- out_weight: bfloat16 [4096, 2880], P('vocab'), may hold values from -0.09375 to 0.09375
- out_bias: float32 [2880], replicated, may hold values from -3 to 3
- residual: bfloat16 [4096, 2880], P('ctx', 'vocab'), may hold values from -3 to 3
- norm_gain: float32 [2880], replicated, may hold values from 0.5 to 1.5
- policy_hidden: bfloat16 [4096, 2880], P('ctx', 'vocab'), may hold values from -6 to 6
- ref_head: bfloat16 [2880, 24576], P(None, 'vocab')
- policy_head: bfloat16 [2880, 24576], P(None, 'vocab')
- token_ids: int32 [4096], P('ctx'), may hold values from 0 to 24575
- advantages: float32 [4096], P('ctx'), may hold values from -8 to 8
- positions: int32 [4096], P('ctx'), may hold values from 0 to 511, as said below
Outputs:
- divergence: float32 [4096], P('ctx')
- hidden_grad: float32 [2880, 4096], P('vocab', 'ctx')
Inputs may be any that keep to these rules, and one draw needn't show every extreme that they name: positions[0] is 0; every other entry is 0, where a document starts, or one more than the entry before it; no document is longer than 512 tokens, and one has exactly 512.
All inputs are finite; a program needn't handle non-finite values.
Results may differ from a plain program's by a relative error of at most 0.02.
Values may be sent and summed in bfloat16 or wider, within the bound.
A program may use at most 128 MiB of HBM per device.

v0:
```python
import jax
import jax.numpy as jnp
from jax import lax
from jax.sharding import PartitionSpec as P

KV_HEADS = 8
HEAD_DIM = 64
WINDOW = 128


def shifted(block, axis, distance):
    devices = range(lax.axis_size(axis))
    route = [(i - distance, i) for i in devices if i - distance in devices]
    return lax.ppermute(block, axis, route)


def shards(
    queries,
    key_rows,
    value_rows,
    sink_logits,
    out_weight,
    out_bias,
    residual,
    norm_gain,
    policy_hidden,
    ref_head,
    policy_head,
    token_ids,
    advantages,
    positions,
):
    row_count = queries.shape[0]
    heads_here = sink_logits.shape[0]
    vocab_index = lax.axis_index("vocab")
    kv_index = vocab_index // (lax.axis_size("vocab") // KV_HEADS)
    key_head = lax.dynamic_slice_in_dim(key_rows, kv_index * HEAD_DIM, HEAD_DIM, 1)
    value_head = lax.dynamic_slice_in_dim(value_rows, kv_index * HEAD_DIM, HEAD_DIM, 1)
    packed = jnp.concatenate([key_head, value_head], axis=1)
    carried = shifted(packed[row_count - WINDOW :], "ctx", 1)
    joined = jnp.concatenate([carried, packed], axis=0)
    key_all = joined[:, :HEAD_DIM]
    value_all = joined[:, HEAD_DIM:]
    query_block = queries.reshape(row_count, heads_here, HEAD_DIM)
    scores = jnp.einsum(
        "rhd,kd->hrk", query_block, key_all, preferred_element_type=jnp.float32
    ) * HEAD_DIM ** (-0.5)
    offsets = jnp.arange(row_count)[:, None] + WINDOW - jnp.arange(row_count + WINDOW)[None, :]
    allowed = (offsets >= 0) & (offsets < WINDOW) & (positions[:, None] >= offsets)
    scores = jnp.where(allowed[None], scores, -jnp.inf)
    peak = jnp.maximum(jnp.max(scores, axis=2), sink_logits[:, None])
    raised = jnp.exp(scores - peak[:, :, None])
    totals = jnp.sum(raised, axis=2) + jnp.exp(sink_logits[:, None] - peak)
    weights = (raised / totals[:, :, None]).astype(jnp.bfloat16)
    mixed = jnp.einsum("hrk,kd->rhd", weights, value_all, preferred_element_type=jnp.float32)
    attended = mixed.reshape(row_count, heads_here * HEAD_DIM).astype(jnp.bfloat16)
    partial_value = jnp.dot(attended, out_weight, preferred_element_type=jnp.float32)
    share = residual.shape[1]
    col_start = vocab_index * share
    own_cols = lax.dynamic_slice_in_dim(partial_value, col_start, share, 1) + residual.astype(
        jnp.float32
    )
    term = lax.dynamic_update_slice_in_dim(partial_value, own_cols, col_start, 1)
    summed = lax.psum(term, "vocab")
    ref_hidden = (summed + out_bias).astype(jnp.bfloat16)
    policy_rows = lax.all_gather(policy_hidden, "vocab", axis=1, tiled=True)
    hidden_wide = ref_hidden.astype(jnp.float32)
    spread = jnp.mean(hidden_wide * hidden_wide, axis=1, keepdims=True)
    ref_normed = (hidden_wide * lax.rsqrt(spread + 1e-05) * norm_gain).astype(jnp.bfloat16)
    ref_logits = jnp.dot(ref_normed, ref_head, preferred_element_type=jnp.float32)
    policy_logits = jnp.dot(policy_rows, policy_head, preferred_element_type=jnp.float32)
    vocab_here = policy_head.shape[1]
    top_policy, top_ref = lax.pmax(
        (jnp.max(policy_logits, axis=1), jnp.max(ref_logits, axis=1)), "vocab"
    )
    exp_policy = jnp.exp(policy_logits - top_policy[:, None])
    exp_ref = jnp.exp(ref_logits - top_ref[:, None])
    total_policy, total_ref = lax.psum(
        (jnp.sum(exp_policy, axis=1), jnp.sum(exp_ref, axis=1)), "vocab"
    )
    log_policy = policy_logits - (top_policy + jnp.log(total_policy))[:, None]
    log_ref = ref_logits - (top_ref + jnp.log(total_ref))[:, None]
    prob = jnp.exp(log_policy)
    divergence = lax.psum(jnp.sum(prob * (log_policy - log_ref), axis=1), "vocab")
    vocab_ids = jnp.arange(vocab_here, dtype=jnp.int32)[None, :] + vocab_index * vocab_here
    onehot = (vocab_ids == token_ids[:, None]).astype(jnp.float32)
    logit_grad = prob * (log_policy - log_ref - divergence[:, None]) - advantages[:, None] * (
        onehot - prob
    )
    logit_grad = logit_grad.astype(jnp.bfloat16)
    hidden_grad = lax.psum_scatter(
        lax.dot_general(
            policy_head, logit_grad, (((1,), (1,)), ((), ())), preferred_element_type=jnp.float32
        ),
        "vocab",
        scatter_dimension=0,
        tiled=True,
    )
    return (divergence, hidden_grad)


def solution(mesh):
    return jax.shard_map(
        shards,
        mesh=mesh,
        in_specs=(
            P("ctx", "vocab"),
            P("ctx", None),
            P("ctx", None),
            P("vocab"),
            P("vocab", None),
            P(),
            P("ctx", "vocab"),
            P(),
            P("ctx", "vocab"),
            P(None, "vocab"),
            P(None, "vocab"),
            P("ctx"),
            P("ctx"),
            P("ctx"),
        ),
        out_specs=(P("ctx"), P("vocab", "ctx")),
        check_vma=False,
    )
```

profile of v0, /device:TPU:0, one launch (start us, length us, event | category | flops | bytes accessed | tf_op | source)
XLA Modules:
  0.0 414.9 jit_solution(14160744595907139637)
XLA Ops:
  7.2 0.0 copy-start
  7.2 0.0 all-gather.3.cloned.1.call-start
  7.2 0.7 all-gather.3.cloned.1.call-update
  7.9 0.0 all-reduce.6.cloned.1.call-start
  8.0 1.1 constant_dynamic-slice_fusion.1
  9.1 0.1 copy.29
  9.2 0.1 copy.30
  9.3 1.3 collective-permute-start
  10.6 1.1 fusion.21
  11.7 1.1 copy.26
  12.8 0.0 copy-start.6
  12.8 0.0 collective-permute-done
  12.9 1.0 fusion.5
  13.9 0.0 copy-done.6
  13.9 0.1 broadcast_maximum_fusion
  14.0 1.1 fusion.4
  15.1 0.1 exponential_add_fusion
  15.2 1.6 fusion.22
  16.9 0.0 copy-done
  16.9 0.0 copy-start.4
  16.9 0.9 fusion.28
  17.8 0.0 copy-start.1
  17.8 2.6 copy-done.1
  20.4 0.0 copy-done.4
  20.4 0.1 convert_add_fusion
  20.4 2.0 dynamic_update_slice.3
  22.5 0.0 all-reduce.6.cloned.1.call-update
  22.5 37.8 %all-gather.3.cloned.1.call-done = bf16[16,180,512]{2,1,0:T(8,128)(2,1)} async-done(((bf16[1,180,512]{2,1,0:T(8,128)(2,1)}), bf16[16,180,512]{2,1,0:T(8,128)(2,1)}) %all-gather.3.cloned.1.call-update) | async-done | bytes 2949136 | tf_op jit(solution)/shard_map/all_gather | solution.py:66
  60.3 4.3 %reshape.124 = bf16[2880,512]{1,0:T(8,128)(2,1)} reshape(bf16[16,180,512]{2,1,0:T(8,128)(2,1)} %all-gather.3.cloned.1.call-done) | data formatting | bytes 5898240
  64.6 0.0 copy-start.5
  64.6 9.9 %fusion.27 = (f32[512]{0:T(512)S(1)}, f32[512,1536]{1,0:T(8,128)}) fusion(bf16[2880,512]{1,0:T(8,128)(2,1)} %reshape.124, bf16[2880,1536]{1,0:T(8,128)(2,1)} %param.24), kind=kOutput, calls=%fused_computation.53 | convolution fusion | flops 4530634240 | bytes 14944256 | tf_op jit(solution)/shard_map/dot_general | solution.py:71
  74.5 0.0 copy-start.9
  74.5 106.9 %all-reduce.6.cloned.1.call-done = f32[512,2880]{0,1:T(8,128)} async-done(((f32[512,2880]{0,1:T(8,128)}), f32[512,2880]{0,1:T(8,128)}) %all-reduce.6.cloned.1.call-update) | async-done | bytes 5898256 | tf_op jit(solution)/shard_map/psum | solution.py:64
  181.4 0.0 copy-done.5
  181.4 0.0 copy-start.3
  181.4 3.7 fusion.1
  185.0 0.0 copy-done.9
  185.0 0.7 copy-done.3
  185.8 10.7 %fusion.26 = (f32[512]{0:T(512)S(1)}, f32[512,1536]{1,0:T(8,128)}) fusion(bf16[2880,1536]{1,0:T(8,128)(2,1)} %param.23, f32[2880]{0:T(1024)S(1)} %copy-done.9, f32[512]{0:T(512)S(1)} %add_rsqrt_fusion, f32[512,2880]{0,1:T(8,128)S(1)} %copy-done.3, f32[2880]{0:T(1024)S(1)} %copy-done.5), kind=kOutput, calls=%fused_computation.52 | convolution fusion | flops 4539481600 | bytes 17918464 | tf_op jit(solution)/shard_map/dot_general | solution.py:70
  196.4 38.3 %all-reduce.3 = (f32[512]{0:T(512)S(1)}, f32[512]{0:T(512)S(1)}) all-reduce(f32[512]{0:T(512)S(1)} %get-tuple-element.8, f32[512]{0:T(512)S(1)} %get-tuple-element.10), channel_id=1, replica_groups=mesh['ctx'=8,'vocab'=16] {'vocab'}, use_global_device_ids=true, to_apply=%region_9.10 | all-reduce | flops 1024 | bytes 8192 | tf_op jit(solution)/shard_map/pmax | solution.py:73
  234.8 0.0 copy-start.2
  234.8 2.6 exponential_reduce_fusion.1
  237.4 0.2 copy-done.2
  237.6 0.6 exponential_reduce_fusion
  238.2 35.5 %all-reduce.2 = (f32[512]{0:T(512)S(1)}, f32[512]{0:T(512)S(1)}) all-reduce(f32[512]{0:T(512)S(1)} %exponential_reduce_fusion, f32[512]{0:T(512)S(1)} %exponential_reduce_fusion.1), channel_id=1, replica_groups=mesh['ctx'=8,'vocab'=16] {'vocab'}, use_global_device_ids=true, to_apply=%region_11.12 | all-reduce | flops 1024 | bytes 8192 | tf_op jit(solution)/shard_map/psum | solution.py:78
  273.6 0.0 copy-start.10
  273.6 0.0 copy-start.11
  273.7 3.7 multiply_reduce_fusion
  277.4 37.5 %psum.31 = f32[512]{0:T(512)S(1)} all-reduce(f32[512]{0:T(512)S(1)} %multiply_reduce_fusion), channel_id=1, replica_groups=mesh['ctx'=8,'vocab'=16] {'vocab'}, use_global_device_ids=true, to_apply=%region_13.14 | all-reduce | flops 512 | bytes 4096 | tf_op jit(solution)/shard_map/psum | solution.py:84
  314.8 0.0 copy-done.10
  314.8 0.0 copy-done.11
  314.8 0.0 copy-start.7
  314.8 13.1 %convolution_bitcast_fusion = f32[2880,512]{1,0:T(8,128)} fusion(bf16[2880,1536]{1,0:T(8,128)(2,1)} %param.24, f32[512,1536]{1,0:T(8,128)} %get-tuple-element.11, f32[512,1536]{1,0:T(8,128)} %get-tuple-element.9, s32[1536]{0:T(1024)S(1)} %iota_add_fusion, f32[512]{0:T(512)S(1)} %copy-done.10, f32[512]{0:T(512)S(1)} %psum.31, f32[512]{0:T(512)S(1)} %log_add_fusion, ...), kind=kOutput, calls=%fused_computation.9 | convolution fusion | flops 4538499072 | bytes 21053440 | tf_op jit(solution)/shard_map/dot_general | solution.py:92
  328.0 0.0 copy-done.7
  328.0 0.0 copy-start.8
  328.0 69.9 %fusion = f32[192,512]{1,0:T(8,128)S(1)} fusion(f32[2880,512]{1,0:T(8,128)} %convolution_bitcast_fusion), kind=kCustom, calls=%all-reduce-scatter | all-reduce-scatter fusion | flops 1572865 | bytes 6291968
  397.9 3.8 collective-permute-start.1
  401.7 0.0 copy-done.8
  401.7 0.6 dynamic-slice.4
  403.0 3.8 collective-permute-done.1
  406.8 0.5 concatenate.8
  407.3 0.8 constant_dynamic-slice_fusion
  (8 shorter events, 0.1 us)
Async XLA Ops:
  7.2 9.7 %copy-start = (bf16[256,2880]{0,1:T(8,128)(2,1)S(1)}, bf16[256,2880]{0,1:T(8,128)(2,1)}, u32[]{:S(2)}) copy-start(bf16[256,2880]{0,1:T(8,128)(2,1)} %param.18) | copy-start | bytes 4423684
  7.2 53.1 %all-gather.3.cloned.1.call-start = ((), (), s32[]{:S(2)}) async-start(), calls=%async_computation.1 | async-start | bytes 3203072 | tf_op jit(solution)/shard_map/all_gather | solution.py:66
  7.9 173.4 %all-reduce.6.cloned.1.call-start = ((), (), s32[]{:S(2)}) async-start(), calls=%async_computation | async-start | bytes 11796480 | tf_op jit(solution)/shard_map/psum | solution.py:64
  9.3 3.5 collective-permute-start
  12.8 1.1 copy-start.6
  16.9 3.5 copy-start.4
  17.8 2.6 copy-start.1
  64.6 116.7 %copy-start.5 = (f32[2880]{0:T(1024)S(1)}, f32[2880]{0:T(1024)}, u32[]{:S(2)}) copy-start(f32[2880]{0:T(1024)} %param.19) | copy-start | bytes 34564
  74.5 110.6 %copy-start.9 = (f32[2880]{0:T(1024)S(1)}, f32[2880]{0:T(1024)}, u32[]{:S(2)}) copy-start(f32[2880]{0:T(1024)} %param.21) | copy-start | bytes 34564
  181.4 4.4 %copy-start.3 = (f32[512,2880]{0,1:T(8,128)S(1)}, f32[512,2880]{0,1:T(8,128)}, u32[]{:S(2)}) copy-start(f32[512,2880]{0,1:T(8,128)} %all-reduce.6.cloned.1.call-done) | copy-start | bytes 17694724
  234.8 2.8 copy-start.2
  273.6 41.2 %copy-start.10 = (f32[512]{0:T(512)S(1)}, f32[512]{0:T(512)}, u32[]{:S(2)}) copy-start(f32[512]{0:T(512)} %param.26) | copy-start | bytes 6148
  273.6 41.2 %copy-start.11 = (s32[512]{0:T(512)S(1)}, s32[512]{0:T(512)}, u32[]{:S(2)}) copy-start(s32[512]{0:T(512)} %param.25) | copy-start | bytes 6148
  314.8 13.1 %copy-start.7 = (f32[512]{0:T(512)}, f32[512]{0:T(512)S(1)}, u32[]{:S(2)}) copy-start(f32[512]{0:T(512)S(1)} %psum.31) | copy-start | bytes 6148
  328.0 73.7 %copy-start.8 = (u32[128]{0:T(128)S(1)}, u32[128]{0:T(128)}, u32[]{:S(2)}) copy-start(u32[128]{0:T(128)} %constant.49) | copy-start | bytes 1540
  397.9 8.9 %collective-permute-start.1 = (f32[180,512]{1,0:T(8,128)S(1)}, f32[180,512]{1,0:T(8,128)S(1)}, u32[]{:S(2)}, u32[]{:S(2)}) collective-permute-start(f32[180,512]{1,0:T(8,128)S(1)} %slice.14), channel_id=1, source_target_pairs={{0,1},{1,2},{2,3},{3,4},{4,5},{5,6},{6,7},{7,8},{8,9},{9,10},{10,1... | collective-permute-start | bytes 1105928
Sparse Core Ops, SparseCore 0:
  10.2 50.0 all-gather.2
  63.7 117.5 all-reduce.5
where the time goes:
time: 418 us; the launch traced here: 415 us
  blocking collectives  181 us (43%)
  waiting for transfers between devices  149 us (36%)
  matrix products  37.2 us (9%)
  between operations  14.9 us (4%)
  local copies, waits for them, and re-layouts  14.2 us (3%)
  other arithmetic  13 us (3%)
  starting transfers between devices  5.13 us (1%)
    psum x1, waiting for transfers between devices, shards(): summed = lax.psum(term, 'vocab')  107 us
    unnamed x1, blocking collectives  69.9 us
    pmax x1, blocking collectives, shards(): lax.pmax((jnp.max(policy_logits, axis=1), jnp.max(ref_logits, axis=1)), '...  38.3 us
    all_gather x1, waiting for transfers between devices, shards(): policy_rows = lax.all_gather(policy_hidden, 'vocab', axis=1, tiled=True)  37.8 us
    psum x1, blocking collectives, shards(): lax.psum(jnp.sum(prob * (log_policy - log_ref), axis=1), 'vocab')  37.5 us
    psum x1, blocking collectives, shards(): lax.psum((jnp.sum(exp_policy, axis=1), jnp.sum(exp_ref, axis=1)), 'vocab')  35.5 us
    dot_general x1, matrix products, shards(): lax.dot_general(policy_head, logit_grad, (((1,), (1,)), ((), ())), prefer...  13.1 us
    unnamed x32, local copies, waits for them, and re-layouts  11.1 us
  transfers between devices with their start and end apart: 4, of which 3 were waited for; matrix products, arithmetic and copies ran while one was open for 6% of the time, Pallas kernels for 0%

commit v1 on v0

v1 whole, which is shorter than its diff:
```python
import functools

import jax
import jax.numpy as jnp
from jax import lax
from jax.experimental import pallas as pl
from jax.experimental.pallas import tpu as pltpu
from jax.sharding import PartitionSpec as P

MESH = pl.DeviceIdType.MESH
BF = jnp.bfloat16
F32 = jnp.float32
HEAD_DIM = 64
WINDOW = 128
SIDE = 4
GROUP = SIDE * SIDE
HALVES = 2
NT = (((1,), (1,)), ((), ()))


class Pool:
    def __init__(self, send_sems, recv_sems):
        self.send_sems, self.recv_sems = send_sems, recv_sems
        self.copies = []

    def start(self, src, dst, device):
        at = len(self.copies)
        copy = pltpu.make_async_remote_copy(
            src_ref=src,
            dst_ref=dst,
            send_sem=self.send_sems.at[at],
            recv_sem=self.recv_sems.at[at],
            device_id=device,
            device_id_type=MESH,
        )
        copy.start()
        self.copies.append(copy)
        return copy


def add_into(dst, src):
    dst[...] = (dst[...].astype(F32) + src[...].astype(F32)).astype(BF)


class Gather:
    def __init__(self, pool, place, buf, half):
        self.pool, self.place, self.buf, self.half = pool, place, buf, half

    def piece(self, da, db):
        return self.buf.at[self.place.block(da, db)]

    def send(self, piece, da, db):
        return self.pool.start(piece, piece, self.place.device(da, db))

    def s0(self):
        own = self.piece(0, 0)
        self.ap, self.am = self.send(own, 1, 0), self.send(own, -1, 0)
        self.bp0, self.bm0 = self.send(own, 0, 1), self.send(own, 0, -1)

    def s1(self):
        self.ap.wait_recv()
        got = self.piece(-1, 0)
        if self.half == 0:
            self.a2 = self.send(got, 1, 0)
        self.bp1, self.bm1 = self.send(got, 0, 1), self.send(got, 0, -1)

    def s2(self):
        self.am.wait_recv()
        got = self.piece(1, 0)
        if self.half == 1:
            self.a2 = self.send(got, -1, 0)
        self.bp2, self.bm2 = self.send(got, 0, 1), self.send(got, 0, -1)

    def s3(self):
        self.a2.wait_recv()
        got = self.piece(2, 0)
        self.bp3, self.bm3 = self.send(got, 0, 1), self.send(got, 0, -1)

    def s4(self):
        self.bp0.wait_recv()
        self.f0 = self.send(self.piece(0, -1), 0, 1)

    def s5(self):
        self.bp1.wait_recv()
        self.f1 = self.send(self.piece(-1, -1), 0, 1)

    def s6(self):
        self.bm2.wait_recv()
        self.f2 = self.send(self.piece(1, 1), 0, -1)

    def s7(self):
        self.bm3.wait_recv()
        self.f3 = self.send(self.piece(2, 1), 0, -1)

    def s8(self):
        for copy in (self.bm0, self.bm1, self.bp2, self.bp3, self.f0, self.f1, self.f2, self.f3):
            copy.wait_recv()


class Scatter:
    def __init__(self, pool, place, x, tp, tm, fp, fm, y, ta, fap, fam, half):
        self.pool, self.place, self.half = pool, place, half
        self.x, self.tp, self.tm, self.fp, self.fm = x, tp, tm, fp, fm
        self.y, self.ta, self.fap, self.fam = y, ta, fap, fam

    def group(self, db, first, count):
        return self.x.at[pl.ds(SIDE * self.place.along_b(db) + first, count)]

    def far(self):
        to = self.place.device
        self.c_tp = self.pool.start(self.group(2, 0, 2), self.tp, to(0, 1))
        self.c_tm = self.pool.start(self.group(2, 2, 2), self.tm, to(0, -1))

    def near(self):
        to = self.place.device
        self.c_fp2 = self.pool.start(self.group(1, 2, 2), self.fp.at[pl.ds(2, 2)], to(0, 1))
        self.c_fm0 = self.pool.start(self.group(-1, 0, 2), self.fm.at[pl.ds(0, 2)], to(0, -1))

    def pass_on(self):
        to = self.place.device
        self.c_tp.wait_recv()
        add_into(self.group(1, 0, 2), self.tp)
        self.c_fp0 = self.pool.start(self.group(1, 0, 2), self.fp.at[pl.ds(0, 2)], to(0, 1))
        self.c_tm.wait_recv()
        add_into(self.group(-1, 2, 2), self.tm)
        self.c_fm2 = self.pool.start(self.group(-1, 2, 2), self.fm.at[pl.ds(2, 2)], to(0, -1))

    def turn(self):
        to = self.place.device
        for copy in (self.c_fp2, self.c_fm0, self.c_fp0, self.c_fm2):
            copy.wait_recv()
        for i in range(SIDE):
            at = SIDE * self.place.b + i
            self.y[i] = (
                self.x[at].astype(F32) + self.fp[i].astype(F32) + self.fm[i].astype(F32)
            ).astype(BF)
        step = 1 if self.half == 0 else -1
        self.c_ta = self.pool.start(self.y.at[self.place.along_a(2)], self.ta, to(step, 0))
        direct = self.y.at[self.place.along_a(-step)]
        if self.half == 0:
            self.c_fam = self.pool.start(direct, self.fam, to(-1, 0))
        else:
            self.c_fap = self.pool.start(direct, self.fap, to(1, 0))

    def last_hop(self):
        to = self.place.device
        self.c_ta.wait_recv()
        if self.half == 0:
            block = self.y.at[self.place.along_a(1)]
            add_into(block, self.ta)
            self.c_fap = self.pool.start(block, self.fap, to(1, 0))
        else:
            block = self.y.at[self.place.along_a(-1)]
            add_into(block, self.ta)
            self.c_fam = self.pool.start(block, self.fam, to(-1, 0))

    def result(self):
        self.c_fap.wait_recv()
        self.c_fam.wait_recv()
        return (
            self.y[self.place.a].astype(F32)
            + self.fap[...].astype(F32)
            + self.fam[...].astype(F32)
        )


class Place:
    def __init__(self):
        self.ctx, self.vocab = lax.axis_index("ctx"), lax.axis_index("vocab")
        self.z, self.x = self.vocab // SIDE, lax.rem(self.vocab, SIDE)
        self.core = lax.rem(self.ctx, 2)
        self.a = self.x * (1 - self.core) + self.z * self.core
        self.b = self.z * (1 - self.core) + self.x * self.core

    def along_a(self, da):
        return lax.rem(self.a + (da + SIDE), SIDE)

    def along_b(self, db):
        return lax.rem(self.b + (db + SIDE), SIDE)

    def block(self, da, db):
        return SIDE * self.along_b(db) + self.along_a(da)

    def device(self, da, db):
        a, b = self.along_a(da), self.along_b(db)
        return (self.ctx, a * (1 + 3 * self.core) + b * (4 - 3 * self.core))

    def block_of(self, vocab):
        turned = SIDE * lax.rem(vocab, SIDE) + vocab // SIDE
        return vocab * (1 - self.core) + turned * self.core


def column(row):
    return jnp.broadcast_to(row, (128, 128)).T


def kernel(
    queries,
    key_rows,
    value_rows,
    sinks,
    out_weight_hbm,
    bias,
    residual,
    gain,
    policy_hidden,
    ref_head_hbm,
    policy_head_hbm,
    token_ids,
    advantages,
    positions,
    divergence_out,
    grad_out,
    out_weight,
    ref_head,
    policy_head,
    head_blocks,
    kv,
    attended,
    land_policy,
    land_residual,
    residual_own,
    policy_rows,
    normed_rows,
    partial_rows,
    policy_logits,
    ref_logits,
    logit_grad,
    grad_parts,
    pol_max,
    pol_sum,
    stats,
    p_tp,
    p_tm,
    p_fp,
    p_fm,
    p_y,
    p_ta,
    p_fap,
    p_fam,
    g_tp,
    g_tm,
    g_fp,
    g_fm,
    g_y,
    g_ta,
    g_fap,
    g_fam,
    local_sems,
    send_sems,
    recv_sems,
    policy_sems,
    residual_sems,
    stat_sems,
):
    rows, width = attended.shape[0], out_weight.shape[1]
    half_rows = rows // HALVES
    piece = half_rows // GROUP
    share = land_policy.shape[3]
    vocab_here = ref_head.shape[1]
    place = Place()
    me = place.vocab
    own = place.block(0, 0)

    loads = [
        pltpu.make_async_copy(src, dst, local_sems.at[i])
        for i, (src, dst) in enumerate(
            (
                (out_weight_hbm, out_weight),
                (policy_head_hbm, policy_head),
                (ref_head_hbm, ref_head),
            )
        )
    ]
    for load in loads:
        load.start()

    barrier = pltpu.get_barrier_semaphore()
    ctx_count = lax.axis_size("ctx")
    next_ctx = lax.rem(place.ctx + 1, ctx_count)
    last_ctx = lax.rem(place.ctx + ctx_count - 1, ctx_count)
    for other in (next_ctx, last_ctx):
        pl.semaphore_signal(barrier, inc=1, device_id=(other, me), device_id_type=MESH)

    def greet(t, carry):
        pl.semaphore_signal(
            barrier,
            inc=1,
            device_id=(place.ctx, lax.rem(me + t, GROUP)),
            device_id_type=MESH,
        )
        return carry

    lax.fori_loop(1, GROUP, greet, 0)

    kv_lanes = pl.ds(pl.multiple_of(place.z * 128, 128), 128)
    upper = lax.rem(me // 2, 2) == 1
    for source, lane in ((key_rows, 0), (value_rows, HEAD_DIM)):
        pair = source[:, kv_lanes]
        kv[pl.ds(WINDOW, rows), lane : lane + HEAD_DIM] = jnp.where(
            upper, pair[:, HEAD_DIM:], pair[:, :HEAD_DIM]
        )
    own_rows = pl.ds(pl.multiple_of(own * piece, piece), piece)
    land_policy[me] = policy_hidden[:, own_rows, :]
    land_residual[me] = residual[:, own_rows, :]

    pl.semaphore_wait(barrier, GROUP - 1 + 2)

    pool = Pool(send_sems, recv_sems)
    halo = pool.start(kv.at[pl.ds(rows, WINDOW)], kv.at[pl.ds(0, WINDOW)], (next_ctx, me))

    def spread(source, land, sems, t):
        to = lax.rem(me + t, GROUP)
        block = pl.ds(pl.multiple_of(place.block_of(to) * piece, piece), piece)
        return pltpu.make_async_remote_copy(
            src_ref=source.at[:, block, :],
            dst_ref=land.at[me],
            send_sem=sems.at[0, t - 1],
            recv_sem=sems.at[1, t - 1],
            device_id=(place.ctx, to),
            device_id_type=MESH,
        )

    def each_peer(act):
        def body(t, carry):
            act(t)
            return carry

        lax.fori_loop(1, GROUP, body, 0)

    each_peer(lambda t: spread(policy_hidden, land_policy, policy_sems, t).start())
    each_peer(lambda t: spread(residual, land_residual, residual_sems, t).start())

    def attend(block):
        at = block * WINDOW
        keys = kv[at : at + 2 * WINDOW, :HEAD_DIM]
        values = kv[at : at + 2 * WINDOW, HEAD_DIM:]
        query = queries[at : at + WINDOW, :]
        heads = query.shape[1] // HEAD_DIM
        offsets = (
            lax.broadcasted_iota(jnp.int32, (WINDOW, 2 * WINDOW), 0)
            + WINDOW
            - lax.broadcasted_iota(jnp.int32, (WINDOW, 2 * WINDOW), 1)
        )
        where_at = column(positions[block : block + 1, :].astype(F32))
        where_at = jnp.concatenate([where_at, where_at], axis=1)
        allowed = (offsets >= 0) & (offsets < WINDOW) & (where_at >= offsets.astype(F32))
        mixed = []
        for h in range(heads):
            scores = (
                lax.dot_general(
                    query[:, h * HEAD_DIM : (h + 1) * HEAD_DIM],
                    keys,
                    NT,
                    preferred_element_type=F32,
                )
                * HEAD_DIM**-0.5
            )
            scores = jnp.where(allowed, scores, -jnp.inf)
            sink = sinks[h]
            peak = jnp.maximum(jnp.max(scores, axis=1, keepdims=True), sink)
            raised = jnp.exp(scores - peak)
            total = jnp.sum(raised, axis=1, keepdims=True) + jnp.exp(sink - peak)
            weights = (raised / total).astype(BF)
            mixed.append(jnp.dot(weights, values, preferred_element_type=F32).astype(BF))
        attended[at : at + WINDOW, :] = jnp.concatenate(mixed, axis=1)

    def project(half):
        rows_in = attended[half * half_rows : (half + 1) * half_rows, :]
        for start in range(0, width, 512):
            stop = min(start + 512, width)
            partial_rows[half, :, :, start:stop] = (
                jnp.dot(rows_in, out_weight[:, start:stop], preferred_element_type=F32)
                .astype(BF)
                .reshape(GROUP, piece, stop - start)
            )

    policy_ag = [Gather(pool, place, policy_rows.at[h], h) for h in range(HALVES)]
    normed_ag = [Gather(pool, place, normed_rows.at[h], h) for h in range(HALVES)]

    def scatter(x, bufs, h):
        return Scatter(pool, place, x.at[h], *(buf.at[h] for buf in bufs), h)

    p_bufs = (p_tp, p_tm, p_fp, p_fm, p_y, p_ta, p_fap, p_fam)
    g_bufs = (g_tp, g_tm, g_fp, g_fm, g_y, g_ta, g_fap, g_fam)
    partial_rs = [scatter(partial_rows, p_bufs, h) for h in range(HALVES)]
    grad_rs = [scatter(grad_parts, g_bufs, h) for h in range(HALVES)]

    def join(land, h):
        return jnp.concatenate([land[v, h] for v in range(GROUP)], axis=1)

    def normalise(h):
        projected = partial_rs[h].result() + bias[...]
        hidden = (residual_own[h].astype(F32) + projected).astype(BF)
        wide = hidden.astype(F32)
        spread_of = jnp.sum(wide * wide, axis=1, keepdims=True) * (1.0 / width)
        normed_rows[h, own] = (wide * lax.rsqrt(spread_of + 1e-05) * gain[...]).astype(BF)

    def logits(rows_of, head, out, h, tile, tiles=3):
        cols = slice(tile * (vocab_here // tiles), (tile + 1) * (vocab_here // tiles))
        lhs = rows_of[h].reshape(half_rows, width)
        out[h, :, cols] = jnp.dot(lhs, head[:, cols], preferred_element_type=F32)

    def policy_stats(h):
        top = jnp.max(policy_logits[h], axis=1, keepdims=True)
        pol_max[h] = jnp.broadcast_to(top, pol_max.shape[1:])
        pol_sum[h] = jnp.broadcast_to(
            jnp.sum(jnp.exp(policy_logits[h] - top), axis=1, keepdims=True), pol_sum.shape[1:]
        )

    def stat_copy(h, t):
        to = lax.rem(me + t, GROUP)
        return pltpu.make_async_remote_copy(
            src_ref=stats.at[h, me],
            dst_ref=stats.at[h, me],
            send_sem=stat_sems.at[h, 0, t - 1],
            recv_sem=stat_sems.at[h, 1, t - 1],
            device_id=(place.ctx, to),
            device_id_type=MESH,
        )

    def send_stats(h):
        top = jnp.max(ref_logits[h], axis=1, keepdims=True)
        total = jnp.sum(jnp.exp(ref_logits[h] - top), axis=1, keepdims=True)
        pol_top = pol_max[h][:, :1]
        gap = jnp.sum(
            jnp.exp(policy_logits[h] - pol_top) * (policy_logits[h] - ref_logits[h]),
            axis=1,
            keepdims=True,
        )
        lane = lax.broadcasted_iota(jnp.int32, (half_rows, 128), 1)
        packed = jnp.where(lane == 0, pol_max[h], pol_sum[h])
        packed = jnp.where(lane == 2, top, packed)
        packed = jnp.where(lane == 3, total, packed)
        packed = jnp.where(lane == 4, gap, packed)
        stats[h, me] = packed.T[:8, :]
        each_peer(lambda t: stat_copy(h, t).start())

    def loss_gradient(h):
        each_peer(lambda t: stat_copy(h, t).wait_recv())
        pol_tops, pol_sums = stats[h, :, 0, :], stats[h, :, 1, :]
        ref_tops, ref_sums = stats[h, :, 2, :], stats[h, :, 3, :]
        pol_top = jnp.max(pol_tops, axis=0, keepdims=True)
        ref_top = jnp.max(ref_tops, axis=0, keepdims=True)
        scale = jnp.exp(pol_tops - pol_top)
        pol_total = jnp.sum(pol_sums * scale, axis=0, keepdims=True)
        gap = jnp.sum(stats[h, :, 4, :] * scale, axis=0, keepdims=True) / pol_total
        ref_total = jnp.sum(ref_sums * jnp.exp(ref_tops - ref_top), axis=0, keepdims=True)
        log_pol = pol_top + jnp.log(pol_total)
        log_ref = ref_top + jnp.log(ref_total)
        divergence_out[h : h + 1, :] = gap - log_pol + log_ref
        for part in range(half_rows // 128):
            lanes = slice(part * 128, (part + 1) * 128)
            at = h * (half_rows // 128) + part
            here = slice(part * 128, (part + 1) * 128)
            adv_row = advantages[at : at + 1, :]
            log_col = column(log_pol[:, lanes])
            add_col = column(adv_row - gap[:, lanes])
            adv_col = column(adv_row)
            tok_col = column(
                (token_ids[at : at + 1, :] - me * vocab_here).astype(F32)
            )
            for chunk in range(0, vocab_here, 128):
                cols = slice(chunk, chunk + 128)
                ids = (lax.broadcasted_iota(jnp.int32, (128, 128), 1) + chunk).astype(F32)
                pol = policy_logits[h, here, cols]
                prob = jnp.exp(pol - log_col)
                value = prob * (pol - ref_logits[h, here, cols] + add_col)
                logit_grad[h, here, cols] = (
                    value - jnp.where(ids == tok_col, adv_col, 0.0)
                ).astype(BF)

    def gradient(h, db):
        at = pl.ds(SIDE * place.along_b(db), SIDE)
        block_rows = head_blocks.shape[1]
        lhs = head_blocks[at].reshape(SIDE * block_rows, vocab_here)
        grad_parts[h, at] = (
            lax.dot_general(lhs, logit_grad[h], NT, preferred_element_type=F32)
            .astype(BF)
            .reshape(SIDE, block_rows, half_rows)
        )

    def finish(h):
        grad_out[:, h * half_rows : (h + 1) * half_rows] = grad_rs[h].result()[:share, :]

    attend(1)
    halo.wait_recv()
    attend(0)
    each_peer(lambda t: spread(policy_hidden, land_policy, policy_sems, t).wait_recv())
    for h in range(HALVES):
        policy_rows[h, own] = join(land_policy, h)
        policy_ag[h].s0()
    loads[0].wait()
    project(0)
    partial_rs[0].far()
    partial_rs[0].near()
    attend(2)
    attend(3)
    project(1)
    partial_rs[1].far()
    partial_rs[1].near()
    for h in range(HALVES):
        policy_ag[h].s1()
        policy_ag[h].s2()
    for h in range(HALVES):
        partial_rs[h].pass_on()
    for h in range(HALVES):
        policy_ag[h].s4()
        policy_ag[h].s3()
    each_peer(lambda t: spread(residual, land_residual, residual_sems, t).wait_recv())
    for h in range(HALVES):
        residual_own[h] = join(land_residual, h)
    loads[1].wait()
    for d in range(GROUP):
        head_blocks[place.block_of(d), :share, :] = policy_head[d * share : (d + 1) * share, :]
    partial_rs[0].turn()
    partial_rs[1].turn()
    policy_ag[0].s5()
    policy_ag[0].s6()
    partial_rs[0].last_hop()
    partial_rs[1].last_hop()
    policy_ag[0].s7()
    normalise(0)
    normed_ag[0].s0()
    normalise(1)
    normed_ag[1].s0()
    policy_ag[1].s5()
    policy_ag[1].s6()
    policy_ag[1].s7()
    normed_ag[0].s1()
    normed_ag[0].s2()
    normed_ag[1].s1()
    normed_ag[1].s2()
    policy_ag[0].s8()
    logits(policy_rows, policy_head, policy_logits, 0, 0)
    normed_ag[0].s4()
    normed_ag[0].s3()
    logits(policy_rows, policy_head, policy_logits, 0, 1)
    normed_ag[1].s4()
    normed_ag[1].s3()
    normed_ag[0].s5()
    normed_ag[0].s6()
    logits(policy_rows, policy_head, policy_logits, 0, 2)
    normed_ag[0].s7()
    policy_ag[1].s8()
    logits(policy_rows, policy_head, policy_logits, 1, 0)
    normed_ag[1].s5()
    normed_ag[1].s6()
    logits(policy_rows, policy_head, policy_logits, 1, 1)
    normed_ag[1].s7()
    logits(policy_rows, policy_head, policy_logits, 1, 2)
    policy_stats(0)
    policy_stats(1)
    loads[2].wait()
    normed_ag[0].s8()
    for tile in range(3):
        logits(normed_rows, ref_head, ref_logits, 0, tile)
    send_stats(0)
    normed_ag[1].s8()
    logits(normed_rows, ref_head, ref_logits, 1, 0)
    logits(normed_rows, ref_head, ref_logits, 1, 1)
    loss_gradient(0)
    gradient(0, 2)
    grad_rs[0].far()
    gradient(0, 1)
    gradient(0, -1)
    grad_rs[0].near()
    gradient(0, 0)
    logits(normed_rows, ref_head, ref_logits, 1, 2)
    send_stats(1)
    grad_rs[0].pass_on()
    loss_gradient(1)
    gradient(1, 2)
    grad_rs[1].far()
    gradient(1, 1)
    gradient(1, -1)
    grad_rs[1].near()
    grad_rs[0].turn()
    gradient(1, 0)
    grad_rs[0].last_hop()
    grad_rs[1].pass_on()
    finish(0)
    grad_rs[1].turn()
    grad_rs[1].last_hop()
    finish(1)

    for copy in pool.copies:
        copy.wait_send()
    each_peer(lambda t: spread(policy_hidden, land_policy, policy_sems, t).wait_send())
    each_peer(lambda t: spread(residual, land_residual, residual_sems, t).wait_send())
    for h in range(HALVES):
        each_peer(lambda t: stat_copy(h, t).wait_send())


def shards(
    queries,
    key_rows,
    value_rows,
    sink_logits,
    out_weight,
    out_bias,
    residual,
    norm_gain,
    policy_hidden,
    ref_head,
    policy_head,
    token_ids,
    advantages,
    positions,
):
    rows, heads_width = queries.shape
    share = residual.shape[1]
    width, vocab_here = ref_head.shape
    half_rows = rows // HALVES
    piece = half_rows // GROUP
    block_rows = -(-share // 16) * 16
    copies = 1 + HALVES * (15 + 15 + 9 + 9)

    def sums(block):
        return [
            pltpu.VMEM((HALVES, *lead, *block), BF)
            for lead in ((2,), (2,), (SIDE,), (SIDE,), (SIDE,), (), (), ())
        ]

    vmem, hbm = (pl.BlockSpec(memory_space=space) for space in (pltpu.VMEM, pl.ANY))
    smem = pl.BlockSpec(memory_space=pltpu.SMEM)
    divergence, grad = pl.pallas_call(
        kernel,
        out_shape=(
            jax.ShapeDtypeStruct((HALVES, half_rows), F32),
            jax.ShapeDtypeStruct((share, rows), F32),
        ),
        in_specs=[
            vmem, vmem, vmem, smem, hbm, vmem, vmem, vmem, vmem, hbm, hbm, vmem, vmem, vmem,
        ],
        out_specs=(vmem, vmem),
        scratch_shapes=[
            pltpu.VMEM((heads_width, width), BF),
            pltpu.VMEM((width, vocab_here), BF),
            pltpu.VMEM((width, vocab_here), BF),
            pltpu.VMEM((GROUP, block_rows, vocab_here), BF),
            pltpu.VMEM((WINDOW + rows, 2 * HEAD_DIM), BF),
            pltpu.VMEM((rows, heads_width), BF),
            pltpu.VMEM((GROUP, HALVES, piece, share), BF),
            pltpu.VMEM((GROUP, HALVES, piece, share), BF),
            pltpu.VMEM((HALVES, piece, width), BF),
            pltpu.VMEM((HALVES, GROUP, piece, width), BF),
            pltpu.VMEM((HALVES, GROUP, piece, width), BF),
            pltpu.VMEM((HALVES, GROUP, piece, width), BF),
            pltpu.VMEM((HALVES, half_rows, vocab_here), F32),
            pltpu.VMEM((HALVES, half_rows, vocab_here), F32),
            pltpu.VMEM((HALVES, half_rows, vocab_here), BF),
            pltpu.VMEM((HALVES, GROUP, block_rows, half_rows), BF),
            pltpu.VMEM((HALVES, half_rows, 128), F32),
            pltpu.VMEM((HALVES, half_rows, 128), F32),
            pltpu.VMEM((HALVES, GROUP, 8, half_rows), F32),
            *sums((piece, width)),
            *sums((block_rows, half_rows)),
            pltpu.SemaphoreType.DMA((3,)),
            pltpu.SemaphoreType.DMA((copies,)),
            pltpu.SemaphoreType.DMA((copies,)),
            pltpu.SemaphoreType.DMA((2, GROUP - 1)),
            pltpu.SemaphoreType.DMA((2, GROUP - 1)),
            pltpu.SemaphoreType.DMA((HALVES, 2, GROUP - 1)),
        ],
        compiler_params=pltpu.CompilerParams(
            collective_id=0, has_side_effects=True, vmem_limit_bytes=62 << 20
        ),
    )(
        queries,
        key_rows,
        value_rows,
        sink_logits,
        out_weight,
        out_bias.reshape(1, width),
        residual.reshape(HALVES, half_rows, share),
        norm_gain.reshape(1, width),
        policy_hidden.reshape(HALVES, half_rows, share),
        ref_head,
        policy_head,
        token_ids.reshape(rows // 128, 128),
        advantages.reshape(rows // 128, 128),
        positions.reshape(rows // 128, 128),
    )
    return divergence.reshape(rows), grad


def solution(mesh):
    return jax.shard_map(
        shards,
        mesh=mesh,
        in_specs=(
            P("ctx", "vocab"),
            P("ctx", None),
            P("ctx", None),
            P("vocab"),
            P("vocab", None),
            P(),
            P("ctx", "vocab"),
            P(),
            P("ctx", "vocab"),
            P(None, "vocab"),
            P(None, "vocab"),
            P("ctx"),
            P("ctx"),
            P("ctx"),
        ),
        out_specs=(P("ctx"), P("vocab", "ctx")),
        check_vma=False,
    )
```

time: 418 us -> 121 us (0.29)
  blocking collectives: 181 us -> 0 us
  waiting for transfers between devices: 149 us -> 0 us
  Pallas kernels: 0 us -> 108 us
  matrix products: 37.2 us -> 0 us
  between operations: 14.9 us -> 0.64 us
  other arithmetic: 13 us -> 0 us
  starting transfers between devices: 5.13 us -> 0 us
    pallas_call x0 -> x1, Pallas kernels: none -> 108 us  [shards(): pl.pallas_call(kernel, out_shape=(jax.ShapeDtypeStruct((HALVES, half_rows...]
    psum x1 -> x0, waiting for transfers between devices: 107 us -> none  [shards(): summed = lax.psum(term, 'vocab')]
    psum x2 -> x0, blocking collectives: 72.9 us -> none  [the longest x1 37.5 us: shards(): lax.psum(jnp.sum(prob * (log_policy - log_ref), axis=1), 'vocab')]
    unnamed x1 -> x0, blocking collectives: 69.9 us -> none
    pmax x1 -> x0, blocking collectives: 38.3 us -> none  [shards(): lax.pmax((jnp.max(policy_logits, axis=1), jnp.max(ref_logits, axis=1)), '...]
    all_gather x1 -> x0, waiting for transfers between devices: 37.8 us -> none  [shards(): policy_rows = lax.all_gather(policy_hidden, 'vocab', axis=1, tiled=True)]
    dot_general x6 -> x0, matrix products: 37.2 us -> none  [the longest x1 13.1 us: shards(): lax.dot_general(policy_head, logit_grad, (((1,), (1,)), ((), ())), prefer...]
    reduce_sum x5 -> x0, other arithmetic: 11.7 us -> none  [the longest x1 3.72 us: shards(): jnp.sum(prob * (log_policy - log_ref), axis=1)]
  transfers between devices with their start and end apart: 4 -> 0, of which waited for: 3 -> 0; matrix products, arithmetic and copies ran while one was open for 6% -> 0% of each run, Pallas kernels for 0% -> 0%
where the time goes in v1:
time: 121 us; the launch traced here: 120 us
  Pallas kernels  108 us (89%)
  local copies, waits for them, and re-layouts  11.7 us (10%)
    pallas_call x1, Pallas kernels, shards(): pl.pallas_call(kernel, out_shape=(jax.ShapeDtypeStruct((HALVES, half_rows...  108 us
    unnamed x5, local copies, waits for them, and re-layouts  9.12 us

profile of v1, /device:TPU:0, one launch (start us, length us, event | category | flops | bytes accessed | tf_op | source)
XLA Modules:
  0.0 120.0 jit_solution(15707512923514137510)
XLA Ops:
  0.6 1.3 %reshape.28.bias = f32[1,2880]{1,0:T(1,128)} reshape(f32[2880]{0:T(1024)} %param.19) | data formatting | bytes 23040 | tf_op jit(solution)/shard_map/reshape | solution.py:675
  1.9 1.3 %reshape.30.gain = f32[1,2880]{1,0:T(1,128)} reshape(f32[2880]{0:T(1024)} %param.21) | data formatting | bytes 23040 | tf_op jit(solution)/shard_map/reshape | solution.py:677
  3.3 1.8 %copy.16 = bf16[512,180]{1,0:T(8,128)(2,1)} copy(bf16[512,180]{0,1:T(8,128)(2,1)} %param.20) | data formatting | bytes 368640 | tf_op args[6]
  5.0 1.8 %copy.17 = bf16[512,180]{1,0:T(8,128)(2,1)} copy(bf16[512,180]{0,1:T(8,128)(2,1)} %param.22) | data formatting | bytes 368640 | tf_op args[8]
  6.8 2.6 %copy.18.out_weight_hbm = bf16[256,2880]{1,0:T(8,128)(2,1)} copy(bf16[256,2880]{0,1:T(8,128)(2,1)} %param.18) | data formatting | bytes 2949120 | tf_op args[4]
  9.4 107.6 %shard_map.149 = (f32[2,256]{1,0:T(2,128)}, f32[180,512]{1,0:T(8,128)}) custom-call(bf16[512,256]{1,0:T(8,128)(2,1)} %queries.1, bf16[512,512]{1,0:T(8,128)(2,1)} %key_rows.1, bf16[512,512]{1,0:T(8,128)(2,1)} %value_rows.1, f32[4]{0:T(128)} %sinks.1, bf16[256,2880]{1,0:T(8,128)(2,1)} %copy.18.out_weight_hbm, f32[1,2880]{1,0:T(1,128)} %reshape.28.bias, ...), custom_call_target="tpu_custom_call" | custom-call | tf_op jit(solution)/shard_map/pallas_call | solution.py:627
  117.0 1.3 %copy.19 = f32[1,2,2,128]{3,1,2,0:T(2,128)} copy(f32[1,2,2,128]{3,2,1,0:T(2,128)} %bitcast.13) | data formatting | bytes 4096
  118.3 1.8 %copy.21 = f32[180,512]{1,0:T(8,128)} copy(f32[180,512]{1,0:T(8,128)} %get-tuple-element.9) | data formatting | bytes 737280

commit v2 on v1

--- a/solution.py
+++ b/solution.py
@@ -98,70 +98,59 @@
 
 
 class Scatter:
-    def __init__(self, pool, place, x, tp, tm, fp, fm, y, ta, fap, fam, half):
-        self.pool, self.place, self.half = pool, place, half
+    def __init__(self, pool, place, x, tp, tm, fp, fm, y, fa):
+        self.pool, self.place = pool, place
         self.x, self.tp, self.tm, self.fp, self.fm = x, tp, tm, fp, fm
-        self.y, self.ta, self.fap, self.fam = y, ta, fap, fam
+        self.y, self.fa = y, fa
 
     def group(self, db, first, count):
         return self.x.at[pl.ds(SIDE * self.place.along_b(db) + first, count)]
 
+    def send(self, src, dst, db):
+        return self.pool.start(src, dst, self.place.device(0, db))
+
     def far(self):
-        to = self.place.device
-        self.c_tp = self.pool.start(self.group(2, 0, 2), self.tp, to(0, 1))
-        self.c_tm = self.pool.start(self.group(2, 2, 2), self.tm, to(0, -1))
-
-    def near(self):
-        to = self.place.device
-        self.c_fp2 = self.pool.start(self.group(1, 2, 2), self.fp.at[pl.ds(2, 2)], to(0, 1))
-        self.c_fm0 = self.pool.start(self.group(-1, 0, 2), self.fm.at[pl.ds(0, 2)], to(0, -1))
+        self.c_tp = self.send(self.group(2, 0, 2), self.tp, 1)
+        self.c_tm = self.send(self.group(2, 2, 2), self.tm, -1)
+
+    def near_up(self):
+        self.c_fp2 = self.send(self.group(1, 2, 2), self.fp.at[pl.ds(2, 2)], 1)
+
+    def near_down(self):
+        self.c_fm0 = self.send(self.group(-1, 0, 2), self.fm.at[pl.ds(0, 2)], -1)
 
     def pass_on(self):
-        to = self.place.device
         self.c_tp.wait_recv()
         add_into(self.group(1, 0, 2), self.tp)
-        self.c_fp0 = self.pool.start(self.group(1, 0, 2), self.fp.at[pl.ds(0, 2)], to(0, 1))
+        self.c_fp0 = self.send(self.group(1, 0, 2), self.fp.at[pl.ds(0, 2)], 1)
         self.c_tm.wait_recv()
         add_into(self.group(-1, 2, 2), self.tm)
-        self.c_fm2 = self.pool.start(self.group(-1, 2, 2), self.fm.at[pl.ds(2, 2)], to(0, -1))
+        self.c_fm2 = self.send(self.group(-1, 2, 2), self.fm.at[pl.ds(2, 2)], -1)
+
+    def here(self, i):
+        return (
+            self.x[SIDE * self.place.b + i].astype(F32)
+            + self.fp[i].astype(F32)
+            + self.fm[i].astype(F32)
+        )
 
     def turn(self):
-        to = self.place.device
         for copy in (self.c_fp2, self.c_fm0, self.c_fp0, self.c_fm2):
             copy.wait_recv()
-        for i in range(SIDE):
-            at = SIDE * self.place.b + i
-            self.y[i] = (
-                self.x[at].astype(F32) + self.fp[i].astype(F32) + self.fm[i].astype(F32)
-            ).astype(BF)
-        step = 1 if self.half == 0 else -1
-        self.c_ta = self.pool.start(self.y.at[self.place.along_a(2)], self.ta, to(step, 0))
-        direct = self.y.at[self.place.along_a(-step)]
-        if self.half == 0:
-            self.c_fam = self.pool.start(direct, self.fam, to(-1, 0))
-        else:
-            self.c_fap = self.pool.start(direct, self.fap, to(1, 0))
-
-    def last_hop(self):
-        to = self.place.device
-        self.c_ta.wait_recv()
-        if self.half == 0:
-            block = self.y.at[self.place.along_a(1)]
-            add_into(block, self.ta)
-            self.c_fap = self.pool.start(block, self.fap, to(1, 0))
-        else:
-            block = self.y.at[self.place.along_a(-1)]
-            add_into(block, self.ta)
-            self.c_fam = self.pool.start(block, self.fam, to(-1, 0))
+        self.c_fa = []
+        for slot, da in enumerate((2, 1, -1)):
+            to = self.place.along_a(da)
+            self.y[slot] = self.here(to).astype(BF)
+            self.c_fa.append(
+                self.pool.start(self.y.at[slot], self.fa.at[slot], self.place.device(da, 0))
+            )
 
     def result(self):
-        self.c_fap.wait_recv()
-        self.c_fam.wait_recv()
-        return (
-            self.y[self.place.a].astype(F32)
-            + self.fap[...].astype(F32)
-            + self.fam[...].astype(F32)
-        )
+        total = self.here(self.place.a)
+        for slot in range(SIDE - 1):
+            self.c_fa[slot].wait_recv()
+            total = total + self.fa[slot].astype(F32)
+        return total
 
 
 class Place:
@@ -195,15 +184,15 @@
 
 
 def kernel(
-    queries,
-    key_rows,
-    value_rows,
+    queries_hbm,
+    key_rows_hbm,
+    value_rows_hbm,
     sinks,
     out_weight_hbm,
     bias,
-    residual,
+    residual_hbm,
     gain,
-    policy_hidden,
+    policy_hidden_hbm,
     ref_head_hbm,
     policy_head_hbm,
     token_ids,
@@ -215,6 +204,13 @@
     ref_head,
     policy_head,
     head_blocks,
+    queries,
+    key_pair,
+    value_pair,
+    policy_turned,
+    residual_turned,
+    policy_hidden,
+    residual,
     kv,
     attended,
     land_policy,
@@ -235,17 +231,13 @@
     p_fp,
     p_fm,
     p_y,
-    p_ta,
-    p_fap,
-    p_fam,
+    p_fa,
     g_tp,
     g_tm,
     g_fp,
     g_fm,
     g_y,
-    g_ta,
-    g_fap,
-    g_fam,
+    g_fa,
     local_sems,
     send_sems,
     recv_sems,
@@ -253,7 +245,7 @@
     residual_sems,
     stat_sems,
 ):
-    rows, width = attended.shape[0], out_weight.shape[1]
+    rows, width = attended.shape[0], out_weight.shape[0]
     half_rows = rows // HALVES
     piece = half_rows // GROUP
     share = land_policy.shape[3]
@@ -262,16 +254,23 @@
     me = place.vocab
     own = place.block(0, 0)
 
+    kv_lanes = pl.ds(pl.multiple_of(place.z * 128, 128), 128)
     loads = [
         pltpu.make_async_copy(src, dst, local_sems.at[i])
         for i, (src, dst) in enumerate(
             (
+                (policy_hidden_hbm, policy_turned),
+                (key_rows_hbm.at[:, kv_lanes], key_pair),
+                (value_rows_hbm.at[:, kv_lanes], value_pair),
+                (queries_hbm, queries),
                 (out_weight_hbm, out_weight),
+                (residual_hbm, residual_turned),
                 (policy_head_hbm, policy_head),
                 (ref_head_hbm, ref_head),
             )
         )
     ]
+    l_policy, l_key, l_value, l_query, l_out, l_residual, l_policy_head, l_ref_head = loads
     for load in loads:
         load.start()
 
@@ -293,16 +292,23 @@
 
     lax.fori_loop(1, GROUP, greet, 0)
 
-    kv_lanes = pl.ds(pl.multiple_of(place.z * 128, 128), 128)
+    own_rows = pl.ds(pl.multiple_of(own * piece, piece), piece)
+
+    def turn_over(source, out, land):
+        for h in range(HALVES):
+            out[h] = source[:, h * half_rows : (h + 1) * half_rows].T
+        land[me] = out[:, own_rows, :]
+
+    l_policy.wait()
+    turn_over(policy_turned, policy_hidden, land_policy)
+
     upper = lax.rem(me // 2, 2) == 1
-    for source, lane in ((key_rows, 0), (value_rows, HEAD_DIM)):
-        pair = source[:, kv_lanes]
+    l_key.wait()
+    l_value.wait()
+    for pair, lane in ((key_pair, 0), (value_pair, HEAD_DIM)):
         kv[pl.ds(WINDOW, rows), lane : lane + HEAD_DIM] = jnp.where(
             upper, pair[:, HEAD_DIM:], pair[:, :HEAD_DIM]
         )
-    own_rows = pl.ds(pl.multiple_of(own * piece, piece), piece)
-    land_policy[me] = policy_hidden[:, own_rows, :]
-    land_residual[me] = residual[:, own_rows, :]
 
     pl.semaphore_wait(barrier, GROUP - 1 + 2)
 
@@ -329,7 +335,6 @@
         lax.fori_loop(1, GROUP, body, 0)
 
     each_peer(lambda t: spread(policy_hidden, land_policy, policy_sems, t).start())
-    each_peer(lambda t: spread(residual, land_residual, residual_sems, t).start())
 
     def attend(block):
         at = block * WINDOW
@@ -370,7 +375,9 @@
         for start in range(0, width, 512):
             stop = min(start + 512, width)
             partial_rows[half, :, :, start:stop] = (
-                jnp.dot(rows_in, out_weight[:, start:stop], preferred_element_type=F32)
+                lax.dot_general(
+                    rows_in, out_weight[start:stop, :], NT, preferred_element_type=F32
+                )
                 .astype(BF)
                 .reshape(GROUP, piece, stop - start)
             )
@@ -379,10 +386,10 @@
     normed_ag = [Gather(pool, place, normed_rows.at[h], h) for h in range(HALVES)]
 
     def scatter(x, bufs, h):
-        return Scatter(pool, place, x.at[h], *(buf.at[h] for buf in bufs), h)
-
-    p_bufs = (p_tp, p_tm, p_fp, p_fm, p_y, p_ta, p_fap, p_fam)
-    g_bufs = (g_tp, g_tm, g_fp, g_fm, g_y, g_ta, g_fap, g_fam)
+        return Scatter(pool, place, x.at[h], *(buf.at[h] for buf in bufs))
+
+    p_bufs = (p_tp, p_tm, p_fp, p_fm, p_y, p_fa)
+    g_bufs = (g_tp, g_tm, g_fp, g_fm, g_y, g_fa)
     partial_rs = [scatter(partial_rows, p_bufs, h) for h in range(HALVES)]
     grad_rs = [scatter(grad_parts, g_bufs, h) for h in range(HALVES)]
 
@@ -390,11 +397,11 @@
         return jnp.concatenate([land[v, h] for v in range(GROUP)], axis=1)
 
     def normalise(h):
-        projected = partial_rs[h].result() + bias[...]
+        projected = partial_rs[h].result() + bias[...].reshape(1, width)
         hidden = (residual_own[h].astype(F32) + projected).astype(BF)
         wide = hidden.astype(F32)
         spread_of = jnp.sum(wide * wide, axis=1, keepdims=True) * (1.0 / width)
-        normed_rows[h, own] = (wide * lax.rsqrt(spread_of + 1e-05) * gain[...]).astype(BF)
+        normed_rows[h, own] = (wide * lax.rsqrt(spread_of + 1e-05) * gain[...].reshape(1, width)).astype(BF)
 
     def logits(rows_of, head, out, h, tile, tiles=3):
         cols = slice(tile * (vocab_here // tiles), (tile + 1) * (vocab_here // tiles))
@@ -448,11 +455,12 @@
         ref_total = jnp.sum(ref_sums * jnp.exp(ref_tops - ref_top), axis=0, keepdims=True)
         log_pol = pol_top + jnp.log(pol_total)
         log_ref = ref_top + jnp.log(ref_total)
-        divergence_out[h : h + 1, :] = gap - log_pol + log_ref
+        divergence = gap - log_pol + log_ref
         for part in range(half_rows // 128):
             lanes = slice(part * 128, (part + 1) * 128)
             at = h * (half_rows // 128) + part
             here = slice(part * 128, (part + 1) * 128)
+            divergence_out[at : at + 1, :] = divergence[:, lanes]
             adv_row = advantages[at : at + 1, :]
             log_col = column(log_pol[:, lanes])
             add_col = column(adv_row - gap[:, lanes])
@@ -483,106 +491,113 @@
     def finish(h):
         grad_out[:, h * half_rows : (h + 1) * half_rows] = grad_rs[h].result()[:share, :]
 
-    attend(1)
+    one, two = 1, 0
+    l_query.wait()
+    attend(2)
+    attend(3)
+    l_out.wait()
+    project(one)
+    partial_rs[one].far()
+    partial_rs[one].near_up()
+    partial_rs[one].near_down()
+    each_peer(lambda t: spread(policy_hidden, land_policy, policy_sems, t).wait_recv())
+    policy_rows[one, own] = join(land_policy, one)
+    policy_ag[one].s0()
     halo.wait_recv()
     attend(0)
-    each_peer(lambda t: spread(policy_hidden, land_policy, policy_sems, t).wait_recv())
-    for h in range(HALVES):
-        policy_rows[h, own] = join(land_policy, h)
-        policy_ag[h].s0()
-    loads[0].wait()
-    project(0)
-    partial_rs[0].far()
-    partial_rs[0].near()
-    attend(2)
-    attend(3)
-    project(1)
-    partial_rs[1].far()
-    partial_rs[1].near()
-    for h in range(HALVES):
-        policy_ag[h].s1()
-        policy_ag[h].s2()
-    for h in range(HALVES):
-        partial_rs[h].pass_on()
-    for h in range(HALVES):
-        policy_ag[h].s4()
-        policy_ag[h].s3()
+    attend(1)
+    project(two)
+    partial_rs[two].far()
+    partial_rs[two].near_up()
+    partial_rs[two].near_down()
+    l_residual.wait()
+    turn_over(residual_turned, residual, land_residual)
+    each_peer(lambda t: spread(residual, land_residual, residual_sems, t).start())
+    partial_rs[one].pass_on()
+    policy_ag[one].s1()
+    policy_ag[one].s2()
+    policy_rows[two, own] = join(land_policy, two)
+    partial_rs[two].pass_on()
+    policy_ag[one].s4()
+    policy_ag[one].s3()
     each_peer(lambda t: spread(residual, land_residual, residual_sems, t).wait_recv())
-    for h in range(HALVES):
-        residual_own[h] = join(land_residual, h)
-    loads[1].wait()
+    residual_own[one] = join(land_residual, one)
+    partial_rs[one].turn()
+    residual_own[two] = join(land_residual, two)
+    policy_ag[one].s5()
+    policy_ag[one].s6()
+    normalise(one)
+    normed_ag[one].s0()
+    partial_rs[two].turn()
+    policy_ag[one].s7()
+    policy_ag[two].s0()
+    normed_ag[one].s1()
+    normed_ag[one].s2()
+    normalise(two)
+    normed_ag[two].s0()
+    normed_ag[one].s4()
+    normed_ag[one].s3()
+    policy_ag[two].s1()
+    policy_ag[two].s2()
+    l_policy_head.wait()
     for d in range(GROUP):
         head_blocks[place.block_of(d), :share, :] = policy_head[d * share : (d + 1) * share, :]
-    partial_rs[0].turn()
-    partial_rs[1].turn()
-    policy_ag[0].s5()
-    policy_ag[0].s6()
-    partial_rs[0].last_hop()
-    partial_rs[1].last_hop()
-    policy_ag[0].s7()
-    normalise(0)
-    normed_ag[0].s0()
-    normalise(1)
-    normed_ag[1].s0()
-    policy_ag[1].s5()
-    policy_ag[1].s6()
-    policy_ag[1].s7()
-    normed_ag[0].s1()
-    normed_ag[0].s2()
-    normed_ag[1].s1()
-    normed_ag[1].s2()
-    policy_ag[0].s8()
-    logits(policy_rows, policy_head, policy_logits, 0, 0)
-    normed_ag[0].s4()
-    normed_ag[0].s3()
-    logits(policy_rows, policy_head, policy_logits, 0, 1)
-    normed_ag[1].s4()
-    normed_ag[1].s3()
-    normed_ag[0].s5()
-    normed_ag[0].s6()
-    logits(policy_rows, policy_head, policy_logits, 0, 2)
-    normed_ag[0].s7()
-    policy_ag[1].s8()
-    logits(policy_rows, policy_head, policy_logits, 1, 0)
-    normed_ag[1].s5()
-    normed_ag[1].s6()
-    logits(policy_rows, policy_head, policy_logits, 1, 1)
-    normed_ag[1].s7()
-    logits(policy_rows, policy_head, policy_logits, 1, 2)
-    policy_stats(0)
-    policy_stats(1)
-    loads[2].wait()
-    normed_ag[0].s8()
+    normed_ag[one].s5()
+    normed_ag[one].s6()
+    normed_ag[one].s7()
+    policy_ag[one].s8()
+    logits(policy_rows, policy_head, policy_logits, one, 0)
+    policy_ag[two].s4()
+    policy_ag[two].s3()
+    normed_ag[two].s1()
+    normed_ag[two].s2()
+    logits(policy_rows, policy_head, policy_logits, one, 1)
+    policy_ag[two].s5()
+    policy_ag[two].s6()
+    policy_ag[two].s7()
+    normed_ag[two].s4()
+    normed_ag[two].s3()
+    logits(policy_rows, policy_head, policy_logits, one, 2)
+    normed_ag[two].s5()
+    normed_ag[two].s6()
+    policy_stats(one)
+    normed_ag[two].s7()
+    normed_ag[one].s8()
+    l_ref_head.wait()
     for tile in range(3):
-        logits(normed_rows, ref_head, ref_logits, 0, tile)
-    send_stats(0)
-    normed_ag[1].s8()
-    logits(normed_rows, ref_head, ref_logits, 1, 0)
-    logits(normed_rows, ref_head, ref_logits, 1, 1)
-    loss_gradient(0)
-    gradient(0, 2)
-    grad_rs[0].far()
-    gradient(0, 1)
-    gradient(0, -1)
-    grad_rs[0].near()
-    gradient(0, 0)
-    logits(normed_rows, ref_head, ref_logits, 1, 2)
-    send_stats(1)
-    grad_rs[0].pass_on()
-    loss_gradient(1)
-    gradient(1, 2)
-    grad_rs[1].far()
-    gradient(1, 1)
-    gradient(1, -1)
-    grad_rs[1].near()
-    grad_rs[0].turn()
-    gradient(1, 0)
-    grad_rs[0].last_hop()
-    grad_rs[1].pass_on()
-    finish(0)
-    grad_rs[1].turn()
-    grad_rs[1].last_hop()
-    finish(1)
+        logits(normed_rows, ref_head, ref_logits, one, tile)
+    send_stats(one)
+    policy_ag[two].s8()
+    logits(policy_rows, policy_head, policy_logits, two, 0)
+    logits(policy_rows, policy_head, policy_logits, two, 1)
+    loss_gradient(one)
+    gradient(one, 2)
+    grad_rs[one].far()
+    gradient(one, 1)
+    grad_rs[one].near_up()
+    gradient(one, -1)
+    grad_rs[one].near_down()
+    logits(policy_rows, policy_head, policy_logits, two, 2)
+    grad_rs[one].pass_on()
+    normed_ag[two].s8()
+    for tile in range(3):
+        logits(normed_rows, ref_head, ref_logits, two, tile)
+    policy_stats(two)
+    send_stats(two)
+    gradient(one, 0)
+    grad_rs[one].turn()
+    loss_gradient(two)
+    gradient(two, 2)
+    grad_rs[two].far()
+    gradient(two, 1)
+    grad_rs[two].near_up()
+    gradient(two, -1)
+    grad_rs[two].near_down()
+    gradient(two, 0)
+    finish(one)
+    grad_rs[two].pass_on()
+    grad_rs[two].turn()
+    finish(two)
 
     for copy in pool.copies:
         copy.wait_send()
@@ -614,12 +629,12 @@
     half_rows = rows // HALVES
     piece = half_rows // GROUP
     block_rows = -(-share // 16) * 16
-    copies = 1 + HALVES * (15 + 15 + 9 + 9)
+    copies = 1 + HALVES * 2 * (15 + 9)
 
     def sums(block):
         return [
-            pltpu.VMEM((HALVES, *lead, *block), BF)
-            for lead in ((2,), (2,), (SIDE,), (SIDE,), (SIDE,), (), (), ())
+            pltpu.VMEM((HALVES, lead, *block), BF)
+            for lead in (2, 2, SIDE, SIDE, SIDE - 1, SIDE - 1)
         ]
 
     vmem, hbm = (pl.BlockSpec(memory_space=space) for space in (pltpu.VMEM, pl.ANY))
@@ -627,18 +642,25 @@
     divergence, grad = pl.pallas_call(
         kernel,
         out_shape=(
-            jax.ShapeDtypeStruct((HALVES, half_rows), F32),
+            jax.ShapeDtypeStruct((rows // 128, 128), F32),
             jax.ShapeDtypeStruct((share, rows), F32),
         ),
         in_specs=[
-            vmem, vmem, vmem, smem, hbm, vmem, vmem, vmem, vmem, hbm, hbm, vmem, vmem, vmem,
+            hbm, hbm, hbm, smem, hbm, vmem, hbm, vmem, hbm, hbm, hbm, vmem, vmem, vmem,
         ],
         out_specs=(vmem, vmem),
         scratch_shapes=[
-            pltpu.VMEM((heads_width, width), BF),
+            pltpu.VMEM((width, heads_width), BF),
             pltpu.VMEM((width, vocab_here), BF),
             pltpu.VMEM((width, vocab_here), BF),
             pltpu.VMEM((GROUP, block_rows, vocab_here), BF),
+            pltpu.VMEM((rows, heads_width), BF),
+            pltpu.VMEM((rows, 2 * HEAD_DIM), BF),
+            pltpu.VMEM((rows, 2 * HEAD_DIM), BF),
+            pltpu.VMEM((share, rows), BF),
+            pltpu.VMEM((share, rows), BF),
+            pltpu.VMEM((HALVES, half_rows, share), BF),
+            pltpu.VMEM((HALVES, half_rows, share), BF),
             pltpu.VMEM((WINDOW + rows, 2 * HEAD_DIM), BF),
             pltpu.VMEM((rows, heads_width), BF),
             pltpu.VMEM((GROUP, HALVES, piece, share), BF),
@@ -656,7 +678,7 @@
             pltpu.VMEM((HALVES, GROUP, 8, half_rows), F32),
             *sums((piece, width)),
             *sums((block_rows, half_rows)),
-            pltpu.SemaphoreType.DMA((3,)),
+            pltpu.SemaphoreType.DMA((8,)),
             pltpu.SemaphoreType.DMA((copies,)),
             pltpu.SemaphoreType.DMA((copies,)),
             pltpu.SemaphoreType.DMA((2, GROUP - 1)),
@@ -671,11 +693,11 @@
         key_rows,
         value_rows,
         sink_logits,
-        out_weight,
-        out_bias.reshape(1, width),
-        residual.reshape(HALVES, half_rows, share),
-        norm_gain.reshape(1, width),
-        policy_hidden.reshape(HALVES, half_rows, share),
+        out_weight.T,
+        out_bias,
+        residual.T,
+        norm_gain,
+        policy_hidden.T,
         ref_head,
         policy_head,
         token_ids.reshape(rows // 128, 128),

time: 121 us -> 112 us (0.926)
  local copies, waits for them, and re-layouts: 11.7 us -> 3 us
    unnamed x5 -> x2, local copies, waits for them, and re-layouts: 9.12 us -> 3 us
    reshape x2 -> x0, local copies, waits for them, and re-layouts: 2.62 us -> none  [the longest x1 1.31 us: shards(): out_bias.reshape(1, width)]
where the time goes in v2:
time: 112 us
  Pallas kernels  108 us (96%)
  local copies, waits for them, and re-layouts  3 us (3%)
    pallas_call x1, Pallas kernels, shards(): pl.pallas_call(kernel, out_shape=(jax.ShapeDtypeStruct((rows // 128, 128)...  108 us
    unnamed x2, local copies, waits for them, and re-layouts  3 us

profile of v2, /device:TPU:0, one launch (start us, length us, event | category | flops | bytes accessed | tf_op | source)
XLA Modules:
  0.0 111.7 jit_solution(2078897418776239805)
XLA Ops:
  0.6 108.0 %shard_map.149 = (f32[4,128]{1,0:T(4,128)}, f32[180,512]{1,0:T(8,128)}) custom-call(bf16[512,256]{1,0:T(8,128)(2,1)} %queries_hbm.1, bf16[512,512]{1,0:T(8,128)(2,1)} %key_rows_hbm.1, bf16[512,512]{1,0:T(8,128)(2,1)} %value_rows_hbm.1, f32[4]{0:T(128)} %sinks.1, bf16[2880,256]{1,0:T(8,128)(2,1)} %bitcast.7, f32[2880]{0:T(1024)} %bias.1, ...), custom_call_target="tpu_custom_call" | custom-call | tf_op jit(solution)/shard_map/pallas_call | solution.py:642
  108.7 1.2 %copy.18 = f32[512]{0:T(512)} copy(f32[512]{0:T(512)} %bitcast.13) | data formatting | bytes 4096
  109.9 1.8 %copy.19 = f32[180,512]{1,0:T(8,128)} copy(f32[180,512]{1,0:T(8,128)} %get-tuple-element.9) | data formatting | bytes 737280

commit v3 on v2

--- a/solution.py
+++ b/solution.py
@@ -119,10 +119,12 @@
     def near_down(self):
         self.c_fm0 = self.send(self.group(-1, 0, 2), self.fm.at[pl.ds(0, 2)], -1)
 
-    def pass_on(self):
+    def pass_up(self):
         self.c_tp.wait_recv()
         add_into(self.group(1, 0, 2), self.tp)
         self.c_fp0 = self.send(self.group(1, 0, 2), self.fp.at[pl.ds(0, 2)], 1)
+
+    def pass_down(self):
         self.c_tm.wait_recv()
         add_into(self.group(-1, 2, 2), self.tm)
         self.c_fm2 = self.send(self.group(-1, 2, 2), self.fm.at[pl.ds(2, 2)], -1)
@@ -494,109 +496,115 @@
     one, two = 1, 0
     l_query.wait()
     attend(2)
+    l_residual.wait()
+    turn_over(residual_turned, residual, land_residual)
+    each_peer(lambda t: spread(residual, land_residual, residual_sems, t).start())
     attend(3)
     l_out.wait()
     project(one)
     partial_rs[one].far()
-    partial_rs[one].near_up()
-    partial_rs[one].near_down()
     each_peer(lambda t: spread(policy_hidden, land_policy, policy_sems, t).wait_recv())
     policy_rows[one, own] = join(land_policy, one)
+    partial_rs[one].near_down()
+    partial_rs[one].near_up()
+    policy_rows[two, own] = join(land_policy, two)
     policy_ag[one].s0()
+    partial_rs[one].pass_down()
+    partial_rs[one].pass_up()
     halo.wait_recv()
+    attend(1)
     attend(0)
-    attend(1)
-    project(two)
-    partial_rs[two].far()
-    partial_rs[two].near_up()
-    partial_rs[two].near_down()
-    l_residual.wait()
-    turn_over(residual_turned, residual, land_residual)
-    each_peer(lambda t: spread(residual, land_residual, residual_sems, t).start())
-    partial_rs[one].pass_on()
     policy_ag[one].s1()
     policy_ag[one].s2()
-    policy_rows[two, own] = join(land_policy, two)
-    partial_rs[two].pass_on()
-    policy_ag[one].s4()
-    policy_ag[one].s3()
-    each_peer(lambda t: spread(residual, land_residual, residual_sems, t).wait_recv())
-    residual_own[one] = join(land_residual, one)
-    partial_rs[one].turn()
-    residual_own[two] = join(land_residual, two)
-    policy_ag[one].s5()
-    policy_ag[one].s6()
-    normalise(one)
-    normed_ag[one].s0()
-    partial_rs[two].turn()
-    policy_ag[one].s7()
-    policy_ag[two].s0()
-    normed_ag[one].s1()
-    normed_ag[one].s2()
-    normalise(two)
-    normed_ag[two].s0()
-    normed_ag[one].s4()
-    normed_ag[one].s3()
-    policy_ag[two].s1()
-    policy_ag[two].s2()
     l_policy_head.wait()
     for d in range(GROUP):
         head_blocks[place.block_of(d), :share, :] = policy_head[d * share : (d + 1) * share, :]
+    project(two)
+    policy_ag[two].s0()
+    each_peer(lambda t: spread(residual, land_residual, residual_sems, t).wait_recv())
+    residual_own[two] = join(land_residual, two)
+    residual_own[one] = join(land_residual, one)
+    partial_rs[one].turn()
+    partial_rs[two].near_up()
+    policy_ag[one].s4()
+    partial_rs[two].far()
+    policy_ag[one].s6()
+    policy_ag[one].s3()
+    partial_rs[two].near_down()
+    normalise(one)
+    normed_ag[one].s0()
+    partial_rs[two].pass_up()
+    policy_ag[one].s7()
+    policy_ag[one].s5()
+    normed_ag[one].s4()
+    partial_rs[two].pass_down()
+    normed_ag[one].s2()
+    policy_ag[one].s8()
+    policy_ag[two].s1()
+    normed_ag[one].s1()
+    logits(policy_rows, policy_head, policy_logits, one, 0)
+    normed_ag[one].s3()
+    partial_rs[two].turn()
+    policy_ag[two].s3()
+    logits(policy_rows, policy_head, policy_logits, one, 1)
     normed_ag[one].s5()
     normed_ag[one].s6()
+    logits(policy_rows, policy_head, policy_logits, one, 2)
+    policy_ag[two].s4()
     normed_ag[one].s7()
-    policy_ag[one].s8()
-    logits(policy_rows, policy_head, policy_logits, one, 0)
-    policy_ag[two].s4()
-    policy_ag[two].s3()
-    normed_ag[two].s1()
-    normed_ag[two].s2()
-    logits(policy_rows, policy_head, policy_logits, one, 1)
-    policy_ag[two].s5()
-    policy_ag[two].s6()
+    normalise(two)
+    normed_ag[two].s0()
+    policy_stats(one)
+    policy_ag[two].s2()
     policy_ag[two].s7()
-    normed_ag[two].s4()
-    normed_ag[two].s3()
-    logits(policy_rows, policy_head, policy_logits, one, 2)
-    normed_ag[two].s5()
-    normed_ag[two].s6()
-    policy_stats(one)
-    normed_ag[two].s7()
     normed_ag[one].s8()
     l_ref_head.wait()
-    for tile in range(3):
-        logits(normed_rows, ref_head, ref_logits, one, tile)
+    logits(normed_rows, ref_head, ref_logits, one, 0)
+    policy_ag[two].s5()
+    logits(normed_rows, ref_head, ref_logits, one, 1)
+    normed_ag[two].s1()
+    logits(normed_rows, ref_head, ref_logits, one, 2)
+    policy_ag[two].s6()
     send_stats(one)
+    normed_ag[two].s5()
+    normed_ag[two].s4()
     policy_ag[two].s8()
+    normed_ag[two].s3()
     logits(policy_rows, policy_head, policy_logits, two, 0)
+    normed_ag[two].s2()
     logits(policy_rows, policy_head, policy_logits, two, 1)
+    logits(policy_rows, policy_head, policy_logits, two, 2)
+    normed_ag[two].s6()
+    normed_ag[two].s7()
     loss_gradient(one)
     gradient(one, 2)
     grad_rs[one].far()
+    normed_ag[two].s8()
     gradient(one, 1)
+    policy_stats(two)
     grad_rs[one].near_up()
+    logits(normed_rows, ref_head, ref_logits, two, 0)
+    logits(normed_rows, ref_head, ref_logits, two, 1)
+    logits(normed_rows, ref_head, ref_logits, two, 2)
+    send_stats(two)
     gradient(one, -1)
     grad_rs[one].near_down()
-    logits(policy_rows, policy_head, policy_logits, two, 2)
-    grad_rs[one].pass_on()
-    normed_ag[two].s8()
-    for tile in range(3):
-        logits(normed_rows, ref_head, ref_logits, two, tile)
-    policy_stats(two)
-    send_stats(two)
-    gradient(one, 0)
-    grad_rs[one].turn()
+    grad_rs[one].pass_down()
+    grad_rs[one].pass_up()
     loss_gradient(two)
     gradient(two, 2)
     grad_rs[two].far()
     gradient(two, 1)
+    gradient(two, -1)
     grad_rs[two].near_up()
-    gradient(two, -1)
     grad_rs[two].near_down()
+    grad_rs[two].pass_up()
+    grad_rs[two].pass_down()
+    gradient(one, 0)
     gradient(two, 0)
+    grad_rs[one].turn()
+    grad_rs[two].turn()
     finish(one)
-    grad_rs[two].pass_on()
-    grad_rs[two].turn()
     finish(two)
 
     for copy in pool.copies:

time: 112 us -> 110 us (0.982)
  Pallas kernels: 108 us -> 106 us
    pallas_call x1, Pallas kernels: 108 us -> 106 us  [shards(): pl.pallas_call(kernel, out_shape=(jax.ShapeDtypeStruct((rows // 128, 128)...]
where the time goes in v3:
time: 110 us; the launch traced here: 109 us
  Pallas kernels  106 us (96%)
  local copies, waits for them, and re-layouts  3 us (3%)
    pallas_call x1, Pallas kernels, shards(): pl.pallas_call(kernel, out_shape=(jax.ShapeDtypeStruct((rows // 128, 128)...  106 us
    unnamed x2, local copies, waits for them, and re-layouts  3 us

profile of v3, /device:TPU:0, one launch (start us, length us, event | category | flops | bytes accessed | tf_op | source)
XLA Modules:
  0.0 109.3 jit_solution(18322564331643300147)
XLA Ops:
  0.6 105.7 %shard_map.149 = (f32[4,128]{1,0:T(4,128)}, f32[180,512]{1,0:T(8,128)}) custom-call(bf16[512,256]{1,0:T(8,128)(2,1)} %queries_hbm.1, bf16[512,512]{1,0:T(8,128)(2,1)} %key_rows_hbm.1, bf16[512,512]{1,0:T(8,128)(2,1)} %value_rows_hbm.1, f32[4]{0:T(128)} %sinks.1, bf16[2880,256]{1,0:T(8,128)(2,1)} %bitcast.7, f32[2880]{0:T(1024)} %bias.1, ...), custom_call_target="tpu_custom_call" | custom-call | tf_op jit(solution)/shard_map/pallas_call | solution.py:650
  106.3 1.2 %copy.18 = f32[512]{0:T(512)} copy(f32[512]{0:T(512)} %bitcast.13) | data formatting | bytes 4096
  107.6 1.8 %copy.19 = f32[180,512]{1,0:T(8,128)} copy(f32[180,512]{1,0:T(8,128)} %get-tuple-element.9) | data formatting | bytes 737280

commit v4 on v3

--- a/solution.py
+++ b/solution.py
@@ -337,6 +337,9 @@
         lax.fori_loop(1, GROUP, body, 0)
 
     each_peer(lambda t: spread(policy_hidden, land_policy, policy_sems, t).start())
+    l_residual.wait()
+    turn_over(residual_turned, residual, land_residual)
+    each_peer(lambda t: spread(residual, land_residual, residual_sems, t).start())
 
     def attend(block):
         at = block * WINDOW
@@ -495,113 +498,110 @@
 
     one, two = 1, 0
     l_query.wait()
+    attend(3)
     attend(2)
-    l_residual.wait()
-    turn_over(residual_turned, residual, land_residual)
-    each_peer(lambda t: spread(residual, land_residual, residual_sems, t).start())
-    attend(3)
     l_out.wait()
     project(one)
     partial_rs[one].far()
+    partial_rs[one].near_down()
+    halo.wait_recv()
+    attend(1)
+    partial_rs[one].near_up()
+    attend(0)
+    project(two)
+    partial_rs[two].near_down()
     each_peer(lambda t: spread(policy_hidden, land_policy, policy_sems, t).wait_recv())
     policy_rows[one, own] = join(land_policy, one)
-    partial_rs[one].near_down()
-    partial_rs[one].near_up()
-    policy_rows[two, own] = join(land_policy, two)
     policy_ag[one].s0()
     partial_rs[one].pass_down()
+    each_peer(lambda t: spread(residual, land_residual, residual_sems, t).wait_recv())
+    residual_own[one] = join(land_residual, one)
+    partial_rs[two].far()
     partial_rs[one].pass_up()
-    halo.wait_recv()
-    attend(1)
-    attend(0)
+    residual_own[two] = join(land_residual, two)
+    partial_rs[two].near_up()
+    policy_rows[two, own] = join(land_policy, two)
+    policy_ag[one].s2()
+    policy_ag[two].s0()
+    partial_rs[one].turn()
+    partial_rs[two].pass_down()
+    partial_rs[two].pass_up()
+    policy_ag[two].s2()
+    policy_ag[one].s3()
+    normalise(one)
     policy_ag[one].s1()
-    policy_ag[one].s2()
+    normed_ag[one].s0()
+    partial_rs[two].turn()
+    policy_ag[one].s4()
+    policy_ag[two].s1()
+    normed_ag[one].s2()
+    normed_ag[one].s1()
+    normed_ag[one].s3()
+    normed_ag[one].s4()
+    normalise(two)
+    policy_ag[one].s6()
+    policy_ag[one].s5()
     l_policy_head.wait()
     for d in range(GROUP):
         head_blocks[place.block_of(d), :share, :] = policy_head[d * share : (d + 1) * share, :]
-    project(two)
-    policy_ag[two].s0()
-    each_peer(lambda t: spread(residual, land_residual, residual_sems, t).wait_recv())
-    residual_own[two] = join(land_residual, two)
-    residual_own[one] = join(land_residual, one)
-    partial_rs[one].turn()
-    partial_rs[two].near_up()
-    policy_ag[one].s4()
-    partial_rs[two].far()
-    policy_ag[one].s6()
-    policy_ag[one].s3()
-    partial_rs[two].near_down()
-    normalise(one)
-    normed_ag[one].s0()
-    partial_rs[two].pass_up()
     policy_ag[one].s7()
-    policy_ag[one].s5()
-    normed_ag[one].s4()
-    partial_rs[two].pass_down()
-    normed_ag[one].s2()
+    normed_ag[two].s0()
+    normed_ag[one].s6()
+    normed_ag[one].s5()
+    normed_ag[one].s7()
     policy_ag[one].s8()
-    policy_ag[two].s1()
-    normed_ag[one].s1()
+    normed_ag[two].s1()
     logits(policy_rows, policy_head, policy_logits, one, 0)
-    normed_ag[one].s3()
-    partial_rs[two].turn()
+    policy_ag[two].s5()
     policy_ag[two].s3()
     logits(policy_rows, policy_head, policy_logits, one, 1)
-    normed_ag[one].s5()
-    normed_ag[one].s6()
     logits(policy_rows, policy_head, policy_logits, one, 2)
     policy_ag[two].s4()
-    normed_ag[one].s7()
-    normalise(two)
-    normed_ag[two].s0()
+    normed_ag[one].s8()
+    normed_ag[two].s3()
+    policy_ag[two].s6()
     policy_stats(one)
-    policy_ag[two].s2()
-    policy_ag[two].s7()
-    normed_ag[one].s8()
     l_ref_head.wait()
     logits(normed_rows, ref_head, ref_logits, one, 0)
-    policy_ag[two].s5()
+    normed_ag[two].s2()
+    policy_ag[two].s7()
     logits(normed_rows, ref_head, ref_logits, one, 1)
-    normed_ag[two].s1()
+    normed_ag[two].s7()
     logits(normed_rows, ref_head, ref_logits, one, 2)
-    policy_ag[two].s6()
+    normed_ag[two].s5()
     send_stats(one)
-    normed_ag[two].s5()
     normed_ag[two].s4()
+    normed_ag[two].s6()
     policy_ag[two].s8()
-    normed_ag[two].s3()
     logits(policy_rows, policy_head, policy_logits, two, 0)
-    normed_ag[two].s2()
     logits(policy_rows, policy_head, policy_logits, two, 1)
     logits(policy_rows, policy_head, policy_logits, two, 2)
-    normed_ag[two].s6()
-    normed_ag[two].s7()
-    loss_gradient(one)
-    gradient(one, 2)
-    grad_rs[one].far()
+    policy_stats(two)
     normed_ag[two].s8()
-    gradient(one, 1)
-    policy_stats(two)
-    grad_rs[one].near_up()
     logits(normed_rows, ref_head, ref_logits, two, 0)
     logits(normed_rows, ref_head, ref_logits, two, 1)
     logits(normed_rows, ref_head, ref_logits, two, 2)
     send_stats(two)
+    loss_gradient(one)
+    gradient(one, 2)
+    grad_rs[one].far()
+    gradient(one, 1)
     gradient(one, -1)
+    grad_rs[one].near_up()
     grad_rs[one].near_down()
+    grad_rs[one].pass_up()
     grad_rs[one].pass_down()
-    grad_rs[one].pass_up()
+    gradient(one, 0)
     loss_gradient(two)
     gradient(two, 2)
     grad_rs[two].far()
     gradient(two, 1)
+    grad_rs[two].near_up()
     gradient(two, -1)
-    grad_rs[two].near_up()
+    gradient(two, 0)
     grad_rs[two].near_down()
     grad_rs[two].pass_up()
     grad_rs[two].pass_down()
-    gradient(one, 0)
-    gradient(two, 0)
     grad_rs[one].turn()
     grad_rs[two].turn()
     finish(one)
@@ -613,6 +613,11 @@
     each_peer(lambda t: spread(residual, land_residual, residual_sems, t).wait_send())
     for h in range(HALVES):
         each_peer(lambda t: stat_copy(h, t).wait_send())
+
+
+def hand_over(divergence, grad, divergence_out, grad_out):
+    divergence_out[...] = divergence[...]
+    grad_out[...] = grad[...]
 
 
 def shards(
@@ -712,6 +717,15 @@
         advantages.reshape(rows // 128, 128),
         positions.reshape(rows // 128, 128),
     )
+    divergence, grad = pl.pallas_call(
+        hand_over,
+        out_shape=(
+            jax.ShapeDtypeStruct(divergence.shape, F32),
+            jax.ShapeDtypeStruct(grad.shape, F32),
+        ),
+        in_specs=[vmem, vmem],
+        out_specs=(vmem, vmem),
+    )(divergence, grad)
     return divergence.reshape(rows), grad
 
 

time: 110 us -> 106 us (0.964)
  local copies, waits for them, and re-layouts: 3 us -> 0 us
    unnamed x2 -> x0, local copies, waits for them, and re-layouts: 3 us -> none
    pallas_call x1, Pallas kernels: 106 us -> 104 us  [shards(): pl.pallas_call(kernel, out_shape=(jax.ShapeDtypeStruct((rows // 128, 128)...]
    pallas_call x0 -> x1, Pallas kernels: none -> 1.76 us  [shards(): pl.pallas_call(hand_over, out_shape=(jax.ShapeDtypeStruct(divergence.shap...]
where the time goes in v4:
time: 106 us
  Pallas kernels  105 us (99%)
    pallas_call x1, Pallas kernels, shards(): pl.pallas_call(kernel, out_shape=(jax.ShapeDtypeStruct((rows // 128, 128)...  104 us

profile of v4, /device:TPU:0, one launch (start us, length us, event | category | flops | bytes accessed | tf_op | source)
XLA Modules:
  0.0 106.1 jit_solution(6944103178305838991)
XLA Ops:
  0.6 103.6 %shard_map.149 = (f32[4,128]{1,0:T(4,128)}, f32[180,512]{1,0:T(8,128)}) custom-call(bf16[512,256]{1,0:T(8,128)(2,1)} %queries_hbm.1, bf16[512,512]{1,0:T(8,128)(2,1)} %key_rows_hbm.1, bf16[512,512]{1,0:T(8,128)(2,1)} %value_rows_hbm.1, f32[4]{0:T(128)} %sinks.1, bf16[2880,256]{1,0:T(8,128)(2,1)} %bitcast.7, f32[2880]{0:T(1024)} %bias.1, ...), custom_call_target="tpu_custom_call" | custom-call | tf_op jit(solution)/shard_map/pallas_call | solution.py:655
  104.3 1.8 %shard_map.150 = (f32[4,128]{1,0:T(4,128)}, f32[180,512]{1,0:T(8,128)}) custom-call(f32[4,128]{1,0:T(4,128)} %get-tuple-element.6.divergence, f32[180,512]{1,0:T(8,128)} %get-tuple-element.7.grad), custom_call_target="tpu_custom_call" | custom-call | tf_op jit(solution)/shard_map/pallas_call | solution.py:720

commit v5 on v4

--- a/solution.py
+++ b/solution.py
@@ -498,86 +498,86 @@
 
     one, two = 1, 0
     l_query.wait()
+    attend(2)
     attend(3)
-    attend(2)
     l_out.wait()
     project(one)
     partial_rs[one].far()
-    partial_rs[one].near_down()
+    l_policy_head.wait()
+    for d in range(GROUP):
+        head_blocks[place.block_of(d), :share, :] = policy_head[d * share : (d + 1) * share, :]
     halo.wait_recv()
     attend(1)
+    partial_rs[one].near_down()
     partial_rs[one].near_up()
     attend(0)
     project(two)
+    partial_rs[two].far()
+    partial_rs[one].pass_up()
+    partial_rs[one].pass_down()
     partial_rs[two].near_down()
     each_peer(lambda t: spread(policy_hidden, land_policy, policy_sems, t).wait_recv())
     policy_rows[one, own] = join(land_policy, one)
     policy_ag[one].s0()
-    partial_rs[one].pass_down()
+    partial_rs[two].pass_down()
+    partial_rs[two].near_up()
+    partial_rs[two].pass_up()
+    partial_rs[one].turn()
     each_peer(lambda t: spread(residual, land_residual, residual_sems, t).wait_recv())
+    residual_own[two] = join(land_residual, two)
+    policy_ag[one].s4()
+    policy_rows[two, own] = join(land_policy, two)
     residual_own[one] = join(land_residual, one)
-    partial_rs[two].far()
-    partial_rs[one].pass_up()
-    residual_own[two] = join(land_residual, two)
-    partial_rs[two].near_up()
-    policy_rows[two, own] = join(land_policy, two)
+    policy_ag[one].s1()
     policy_ag[one].s2()
+    partial_rs[two].turn()
+    normalise(one)
+    normed_ag[one].s0()
+    policy_ag[one].s3()
     policy_ag[two].s0()
-    partial_rs[one].turn()
-    partial_rs[two].pass_down()
-    partial_rs[two].pass_up()
+    normed_ag[one].s2()
+    normalise(two)
+    normed_ag[two].s0()
     policy_ag[two].s2()
-    policy_ag[one].s3()
-    normalise(one)
-    policy_ag[one].s1()
-    normed_ag[one].s0()
-    partial_rs[two].turn()
-    policy_ag[one].s4()
     policy_ag[two].s1()
-    normed_ag[one].s2()
+    policy_ag[one].s7()
+    normed_ag[one].s3()
     normed_ag[one].s1()
-    normed_ag[one].s3()
+    policy_ag[one].s5()
     normed_ag[one].s4()
-    normalise(two)
     policy_ag[one].s6()
-    policy_ag[one].s5()
-    l_policy_head.wait()
-    for d in range(GROUP):
-        head_blocks[place.block_of(d), :share, :] = policy_head[d * share : (d + 1) * share, :]
-    policy_ag[one].s7()
-    normed_ag[two].s0()
     normed_ag[one].s6()
+    normed_ag[two].s1()
     normed_ag[one].s5()
+    policy_ag[two].s3()
+    policy_ag[two].s5()
+    policy_ag[two].s4()
+    normed_ag[two].s4()
     normed_ag[one].s7()
+    normed_ag[two].s2()
+    policy_ag[two].s6()
     policy_ag[one].s8()
-    normed_ag[two].s1()
     logits(policy_rows, policy_head, policy_logits, one, 0)
-    policy_ag[two].s5()
-    policy_ag[two].s3()
     logits(policy_rows, policy_head, policy_logits, one, 1)
+    normed_ag[two].s3()
     logits(policy_rows, policy_head, policy_logits, one, 2)
-    policy_ag[two].s4()
+    policy_ag[two].s7()
+    policy_stats(one)
+    normed_ag[two].s5()
     normed_ag[one].s8()
-    normed_ag[two].s3()
-    policy_ag[two].s6()
-    policy_stats(one)
     l_ref_head.wait()
     logits(normed_rows, ref_head, ref_logits, one, 0)
-    normed_ag[two].s2()
-    policy_ag[two].s7()
+    normed_ag[two].s6()
     logits(normed_rows, ref_head, ref_logits, one, 1)
+    logits(normed_rows, ref_head, ref_logits, one, 2)
     normed_ag[two].s7()
-    logits(normed_rows, ref_head, ref_logits, one, 2)
-    normed_ag[two].s5()
     send_stats(one)
-    normed_ag[two].s4()
-    normed_ag[two].s6()
     policy_ag[two].s8()
     logits(policy_rows, policy_head, policy_logits, two, 0)
     logits(policy_rows, policy_head, policy_logits, two, 1)
     logits(policy_rows, policy_head, policy_logits, two, 2)
+    normed_ag[two].s8()
     policy_stats(two)
-    normed_ag[two].s8()
     logits(normed_rows, ref_head, ref_logits, two, 0)
     logits(normed_rows, ref_head, ref_logits, two, 1)
     logits(normed_rows, ref_head, ref_logits, two, 2)
@@ -588,21 +588,21 @@
     gradient(one, 1)
     gradient(one, -1)
     grad_rs[one].near_up()
+    gradient(one, 0)
     grad_rs[one].near_down()
     grad_rs[one].pass_up()
     grad_rs[one].pass_down()
-    gradient(one, 0)
     loss_gradient(two)
     gradient(two, 2)
     grad_rs[two].far()
     gradient(two, 1)
+    gradient(two, -1)
     grad_rs[two].near_up()
-    gradient(two, -1)
+    grad_rs[two].near_down()
+    grad_rs[two].pass_down()
+    grad_rs[two].pass_up()
+    grad_rs[one].turn()
     gradient(two, 0)
-    grad_rs[two].near_down()
-    grad_rs[two].pass_up()
-    grad_rs[two].pass_down()
-    grad_rs[one].turn()
     grad_rs[two].turn()
     finish(one)
     finish(two)

time: 106 us -> 101 us (0.953)
  Pallas kernels: 105 us -> 100 us
    pallas_call x1, Pallas kernels: 104 us -> 98.7 us  [shards(): pl.pallas_call(kernel, out_shape=(jax.ShapeDtypeStruct((rows // 128, 128)...]
where the time goes in v5:
time: 101 us
  Pallas kernels  100 us (99%)
    pallas_call x1, Pallas kernels, shards(): pl.pallas_call(kernel, out_shape=(jax.ShapeDtypeStruct((rows // 128, 128)...  98.7 us

profile of v5, /device:TPU:0, one launch (start us, length us, event | category | flops | bytes accessed | tf_op | source)
XLA Modules:
  0.0 101.1 jit_solution(12359621131537655044)
XLA Ops:
  0.6 98.7 %shard_map.149 = (f32[4,128]{1,0:T(4,128)}, f32[180,512]{1,0:T(8,128)}) custom-call(bf16[512,256]{1,0:T(8,128)(2,1)} %queries_hbm.1, bf16[512,512]{1,0:T(8,128)(2,1)} %key_rows_hbm.1, bf16[512,512]{1,0:T(8,128)(2,1)} %value_rows_hbm.1, f32[4]{0:T(128)} %sinks.1, bf16[2880,256]{1,0:T(8,128)(2,1)} %bitcast.7, f32[2880]{0:T(1024)} %bias.1, ...), custom_call_target="tpu_custom_call" | custom-call | tf_op jit(solution)/shard_map/pallas_call | solution.py:655
  99.4 1.8 %shard_map.150 = (f32[4,128]{1,0:T(4,128)}, f32[180,512]{1,0:T(8,128)}) custom-call(f32[4,128]{1,0:T(4,128)} %get-tuple-element.6.divergence, f32[180,512]{1,0:T(8,128)} %get-tuple-element.7.grad), custom_call_target="tpu_custom_call" | custom-call | tf_op jit(solution)/shard_map/pallas_call | solution.py:720
